TPU v7x, 32 devices: a whole 2x2x4 slice. The times are simulated.
32 devices in a mesh: dp: 16 (over z, y, core), fsdp: 2 (over x).
Axes of the slice: x: 2, y: 2, z: 4, core: 2. Of those that a mesh axis runs over, the one named last changes fastest.
Arguments:
- tokens: bfloat16 [32768, 1024], P(('dp', 'fsdp')), may hold values from -6 to 6
- segment_ids: int32 [32768], P(('dp', 'fsdp')), may hold values from 0 to 32, as said below
- positions: int32 [32768], P(('dp', 'fsdp')), may hold values from 0 to 1982, as said below
- attn_gain: bfloat16 [1024], P('fsdp'), may hold values from 0.25 to 1.75
- qkv_weight: bfloat16 [1024, 3072], P('fsdp'), may hold values from -0.1875 to 0.1875
- attn_out_weight: bfloat16 [1024, 1024], P('fsdp'), may hold values from -0.75 to 0.75
- mlp_gain: bfloat16 [1024], P('fsdp'), may hold values from 0.25 to 1.75
- mlp_in_weight: bfloat16 [1024, 5248], P('fsdp'), may hold values from -0.1875 to 0.1875
- mlp_out_weight: bfloat16 [2624, 1024], P('fsdp'), may hold values from -0.125 to 0.125
- out_cotangent: bfloat16 [32768, 1024], P(('dp', 'fsdp')), may hold values from -6 to 6
Outputs:
- layer_out: bfloat16 [32768, 1024], P(('dp', 'fsdp'))
- grad_tokens: float32 [32768, 1024], P(('dp', 'fsdp'))
- grad_attn_gain: float32 [1024], P('fsdp')
- grad_qkv_weight: float32 [1024, 3072], P('fsdp')
- grad_attn_out_weight: float32 [1024, 1024], P('fsdp')
- grad_mlp_gain: float32 [1024], P('fsdp')
- grad_mlp_in_weight: float32 [1024, 5248], P('fsdp')
- grad_mlp_out_weight: float32 [2624, 1024], P('fsdp')
Inputs may be any that keep to these rules, and one draw needn't show every extreme that they name: `segment_ids`: documents are numbered in stream order from 0. Each aligned block of 1024 tokens holds exactly one document start, which lies 64 or more tokens after the block's first token; the stream's first token also starts a document. `positions`: counts tokens since the first token of the token's document, following segment_ids; the longest document holds 1983 tokens.
All inputs are finite; a program needn't handle non-finite values.
Results may differ from a plain program's by a relative error of at most 0.024.
Values may be sent and summed in bfloat16 or wider, within the bound.
A program may use at most 256 MiB of HBM per device.

v0:
```python
import jax
import jax.numpy as jnp
from jax import lax
from jax.sharding import PartitionSpec as P

HEADS = 16
HALF = 64
QBLOCK = 512


EPSILON = 1e-05
MASKED = -1e30


def with_halo(block, sides, width):
    for axis, dim in sides:
        count = lax.axis_size(axis)
        forward = [(i, i + 1) for i in range(count - 1)]
        backward = [(target, source) for source, target in forward]
        low = lax.ppermute(
            lax.slice_in_dim(block, block.shape[dim] - width, None, axis=dim), axis, forward
        )
        high = lax.ppermute(lax.slice_in_dim(block, 0, width, axis=dim), axis, backward)
        block = jnp.concatenate([low, block, high], axis=dim)
    return block


def passed_along(x, axis, by):
    devices = lax.axis_size(axis)
    pairs = [(i, i + by) for i in range(devices) if 0 <= i + by < devices]
    return lax.ppermute(x, axis, pairs)


def norm_forward(values, gain):
    average = jnp.mean(values, axis=-1, keepdims=True)
    centred = values - average
    inverse = lax.rsqrt(jnp.mean(centred * centred, axis=-1, keepdims=True) + EPSILON)
    scaled = centred * inverse
    return (scaled * gain, scaled, inverse)


def norm_backward(incoming, gain, scaled, inverse):
    weighted = incoming * gain
    inner = weighted - jnp.mean(weighted, axis=-1, keepdims=True)
    inner = inner - scaled * jnp.mean(weighted * scaled, axis=-1, keepdims=True)
    return (inner * inverse, jnp.sum(incoming * scaled, axis=0))


def rotate(values, cosine_table, sine_table, direction):
    half_dim = values.shape[-1] // 2
    first_half = values[..., :half_dim]
    second_half = values[..., half_dim:]
    return jnp.concatenate(
        [
            first_half * cosine_table - direction * second_half * sine_table,
            second_half * cosine_table + direction * first_half * sine_table,
        ],
        axis=-1,
    )


def exact_gelu(values):
    return jax.nn.gelu(values, approximate=False)


def body(
    tokens,
    segment_ids,
    positions,
    attn_gain,
    qkv_weight,
    attn_out_weight,
    mlp_gain,
    mlp_in_weight,
    mlp_out_weight,
    out_cotangent,
):
    weights = (attn_gain, qkv_weight, attn_out_weight, mlp_gain, mlp_in_weight, mlp_out_weight)
    gain_one, w_qkv, w_attn, gain_two, w_in, w_out = (
        lax.all_gather(weights[0], "fsdp", axis=0, tiled=True),
        lax.all_gather(weights[1], "fsdp", axis=0, tiled=True),
        lax.all_gather(weights[2], "fsdp", axis=0, tiled=True),
        lax.all_gather(weights[3], "fsdp", axis=0, tiled=True),
        lax.all_gather(weights[4], "fsdp", axis=0, tiled=True),
        lax.all_gather(weights[5], "fsdp", axis=0, tiled=True),
    )
    rows_here = tokens.shape[0]
    model_width = tokens.shape[1]
    head_dim = model_width // HEADS
    hidden = w_in.shape[1] // 2
    stream_rank = lax.axis_index(("dp", "fsdp"))
    stream_len = rows_here * lax.axis_size(("dp", "fsdp"))
    key_span = QBLOCK + 2 * HALF
    score_scale = 1.0 / head_dim**0.5
    inputs_f = tokens.astype(jnp.float32)
    normed_one, scaled_one, inverse_one = norm_forward(inputs_f, gain_one.astype(jnp.float32))
    act_one = normed_one.astype(jnp.bfloat16)
    qkv = jnp.dot(act_one, w_qkv, preferred_element_type=jnp.float32)
    frequency = jnp.power(10000.0, -jnp.arange(0, head_dim, 2, dtype=jnp.float32) / head_dim)
    angles = positions.astype(jnp.float32)[:, None] * frequency[None, :]
    cosine_table = jnp.cos(angles)[:, None, :]
    sine_table = jnp.sin(angles)[:, None, :]
    query = rotate(
        qkv[:, :model_width].reshape(rows_here, HEADS, head_dim), cosine_table, sine_table, 1.0
    )
    query = query.astype(jnp.bfloat16)
    key_rot = rotate(
        qkv[:, model_width : 2 * model_width].reshape(rows_here, HEADS, head_dim),
        cosine_table,
        sine_table,
        1.0,
    )
    key_value = jnp.concatenate(
        [key_rot.reshape(rows_here, model_width), qkv[:, 2 * model_width :]], axis=1
    ).astype(jnp.bfloat16)
    padded = with_halo(key_value, ((("dp", "fsdp"), 0),), HALF)
    seg_padded = jnp.concatenate(
        [jnp.full((HALF,), -1, jnp.int32), segment_ids, jnp.full((HALF,), -1, jnp.int32)]
    )
    last_segment = segment_ids[rows_here - 1]

    def block_mask(first_row):
        query_index = first_row + jnp.arange(QBLOCK, dtype=jnp.int32)
        key_index = first_row + jnp.arange(key_span, dtype=jnp.int32) - HALF
        seg_query = lax.dynamic_slice_in_dim(segment_ids, first_row, QBLOCK, 0)
        pos_query = lax.dynamic_slice_in_dim(positions, first_row, QBLOCK, 0)
        seg_key = lax.dynamic_slice_in_dim(seg_padded, first_row, key_span, 0)
        nearby = jnp.abs(query_index[:, None] - key_index[None, :]) <= HALF
        global_key = stream_rank * rows_here + key_index
        inside = (global_key >= 0) & (global_key < stream_len)
        earlier_doc = pos_query[:, None] >= query_index[:, None] - key_index[None, :]
        later_doc = jnp.broadcast_to((seg_query == last_segment)[:, None], nearby.shape)
        same_doc = seg_query[:, None] == seg_key[None, :]
        joined = jnp.where(
            key_index[None, :] < 0,
            earlier_doc,
            jnp.where(key_index[None, :] >= rows_here, later_doc, same_doc),
        )
        return nearby & inside[None, :] & joined

    def block_pieces(first_row):
        query_block = lax.dynamic_slice_in_dim(query, first_row, QBLOCK, 0)
        window = lax.dynamic_slice_in_dim(padded, first_row, key_span, 0)
        key_block = window[:, :model_width].reshape(key_span, HEADS, head_dim)
        value_block = window[:, model_width:].reshape(key_span, HEADS, head_dim)
        scores = (
            jnp.einsum("qhd,khd->hqk", query_block, key_block, preferred_element_type=jnp.float32)
            * score_scale
        )
        scores = jnp.where(block_mask(first_row)[None], scores, MASKED)
        return (query_block, key_block, value_block, scores)

    def block_forward(first_row):
        query_block, key_block, value_block, scores = block_pieces(first_row)
        highest = jnp.max(scores, axis=-1, keepdims=True)
        expo_scores = jnp.exp(scores - highest)
        totals = jnp.sum(expo_scores, axis=-1, keepdims=True)
        probs = (expo_scores / totals).astype(jnp.bfloat16)
        mixed_heads = jnp.einsum(
            "hqk,khd->qhd", probs, value_block, preferred_element_type=jnp.float32
        )
        return (mixed_heads.reshape(QBLOCK, model_width), (highest + jnp.log(totals))[..., 0])

    block_rows = jnp.arange(rows_here // QBLOCK, dtype=jnp.int32) * QBLOCK
    attended, log_totals = lax.map(block_forward, block_rows)
    attended = attended.reshape(rows_here, model_width).astype(jnp.bfloat16)
    resid = inputs_f + jnp.dot(attended, w_attn, preferred_element_type=jnp.float32)
    normed_two, scaled_two, inverse_two = norm_forward(resid, gain_two.astype(jnp.float32))
    act_two = normed_two.astype(jnp.bfloat16)
    projected = jnp.dot(act_two, w_in, preferred_element_type=jnp.float32)
    gating = projected[:, hidden:]
    activated, gelu_pullback = jax.vjp(exact_gelu, projected[:, :hidden])
    product = (activated * gating).astype(jnp.bfloat16)
    layer_out = (resid + jnp.dot(product, w_out, preferred_element_type=jnp.float32)).astype(
        jnp.bfloat16
    )
    gain_one, w_qkv, w_attn, gain_two, w_in, w_out = (
        lax.all_gather(weights[0], "fsdp", axis=0, tiled=True),
        lax.all_gather(weights[1], "fsdp", axis=0, tiled=True),
        lax.all_gather(weights[2], "fsdp", axis=0, tiled=True),
        lax.all_gather(weights[3], "fsdp", axis=0, tiled=True),
        lax.all_gather(weights[4], "fsdp", axis=0, tiled=True),
        lax.all_gather(weights[5], "fsdp", axis=0, tiled=True),
    )
    grad_wout = jnp.einsum("nf,nd->fd", product, out_cotangent, preferred_element_type=jnp.float32)
    grad_product = jnp.einsum("nd,fd->nf", out_cotangent, w_out, preferred_element_type=jnp.float32)
    grad_upper = gelu_pullback(grad_product * gating)[0]
    grad_proj = jnp.concatenate([grad_upper, grad_product * activated], axis=1).astype(jnp.bfloat16)
    grad_win = jnp.einsum("nd,nf->df", act_two, grad_proj, preferred_element_type=jnp.float32)
    grad_act_two = jnp.einsum("nf,df->nd", grad_proj, w_in, preferred_element_type=jnp.float32)
    grad_norm_two, grad_gain_two = norm_backward(
        grad_act_two, gain_two.astype(jnp.float32), scaled_two, inverse_two
    )
    grad_resid = out_cotangent.astype(jnp.float32) + grad_norm_two
    grad_mixed = grad_resid.astype(jnp.bfloat16)
    grad_wattn = jnp.einsum("nd,ne->de", attended, grad_mixed, preferred_element_type=jnp.float32)
    grad_attended = jnp.einsum("ne,de->nd", grad_mixed, w_attn, preferred_element_type=jnp.float32)
    grad_attended = grad_attended.astype(jnp.bfloat16).reshape(rows_here, HEADS, head_dim)

    def block_backward(accumulated, inputs):
        first_row, log_total = inputs
        query_block, key_block, value_block, scores = block_pieces(first_row)
        grad_out_block = lax.dynamic_slice_in_dim(grad_attended, first_row, QBLOCK, 0)
        probs = jnp.exp(scores - log_total[..., None])
        grad_probs = jnp.einsum(
            "qhd,khd->hqk", grad_out_block, value_block, preferred_element_type=jnp.float32
        )
        centre = jnp.sum(probs * grad_probs, axis=-1, keepdims=True)
        grad_scores = (probs * (grad_probs - centre)).astype(jnp.bfloat16)
        grad_query_block = (
            jnp.einsum("hqk,khd->qhd", grad_scores, key_block, preferred_element_type=jnp.float32)
            * score_scale
        )
        grad_key_block = (
            jnp.einsum("hqk,qhd->khd", grad_scores, query_block, preferred_element_type=jnp.float32)
            * score_scale
        )
        grad_value_block = jnp.einsum(
            "hqk,qhd->khd",
            probs.astype(jnp.bfloat16),
            grad_out_block,
            preferred_element_type=jnp.float32,
        )
        block_grad = jnp.concatenate(
            [
                grad_key_block.reshape(key_span, model_width),
                grad_value_block.reshape(key_span, model_width),
            ],
            axis=1,
        )
        current = lax.dynamic_slice_in_dim(accumulated, first_row, key_span, 0)
        accumulated = lax.dynamic_update_slice_in_dim(
            accumulated, current + block_grad, first_row, 0
        )
        return (accumulated, grad_query_block.reshape(QBLOCK, model_width))

    empty = jnp.zeros((rows_here + 2 * HALF, 2 * model_width), jnp.float32)
    grad_padded, grad_query = lax.scan(block_backward, empty, (block_rows, log_totals))
    from_above = passed_along(grad_padded[:HALF].astype(jnp.bfloat16), ("dp", "fsdp"), -1).astype(
        jnp.float32
    )
    from_below = passed_along(
        grad_padded[rows_here + HALF :].astype(jnp.bfloat16), ("dp", "fsdp"), 1
    ).astype(jnp.float32)
    grad_pair = grad_padded[HALF : HALF + rows_here]
    grad_pair = grad_pair.at[:HALF].add(from_below).at[rows_here - HALF :].add(from_above)
    grad_query = rotate(
        grad_query.reshape(rows_here, HEADS, head_dim), cosine_table, sine_table, -1.0
    )
    grad_key = rotate(
        grad_pair[:, :model_width].reshape(rows_here, HEADS, head_dim),
        cosine_table,
        sine_table,
        -1.0,
    )
    grad_qkv = jnp.concatenate(
        [
            grad_query.reshape(rows_here, model_width),
            grad_key.reshape(rows_here, model_width),
            grad_pair[:, model_width:],
        ],
        axis=1,
    ).astype(jnp.bfloat16)
    grad_wqkv = jnp.einsum("nd,nf->df", act_one, grad_qkv, preferred_element_type=jnp.float32)
    grad_act_one = jnp.einsum("nf,df->nd", grad_qkv, w_qkv, preferred_element_type=jnp.float32)
    grad_norm_one, grad_gain_one = norm_backward(
        grad_act_one, gain_one.astype(jnp.float32), scaled_one, inverse_one
    )
    grad_tokens = grad_resid + grad_norm_one
    gradients = (grad_gain_one, grad_wqkv, grad_wattn, grad_gain_two, grad_win, grad_wout)
    shards = (
        lax.psum_scatter(
            gradients[0].astype(jnp.bfloat16), "fsdp", scatter_dimension=0, tiled=True
        ).astype(jnp.float32),
        lax.psum_scatter(
            gradients[1].astype(jnp.bfloat16), "fsdp", scatter_dimension=0, tiled=True
        ).astype(jnp.float32),
        lax.psum_scatter(
            gradients[2].astype(jnp.bfloat16), "fsdp", scatter_dimension=0, tiled=True
        ).astype(jnp.float32),
        lax.psum_scatter(
            gradients[3].astype(jnp.bfloat16), "fsdp", scatter_dimension=0, tiled=True
        ).astype(jnp.float32),
        lax.psum_scatter(
            gradients[4].astype(jnp.bfloat16), "fsdp", scatter_dimension=0, tiled=True
        ).astype(jnp.float32),
        lax.psum_scatter(
            gradients[5].astype(jnp.bfloat16), "fsdp", scatter_dimension=0, tiled=True
        ).astype(jnp.float32),
    )
    shards = (
        lax.psum(shards[0].astype(jnp.bfloat16), "dp").astype(jnp.float32),
        lax.psum(shards[1].astype(jnp.bfloat16), "dp").astype(jnp.float32),
        lax.psum(shards[2].astype(jnp.bfloat16), "dp").astype(jnp.float32),
        lax.psum(shards[3].astype(jnp.bfloat16), "dp").astype(jnp.float32),
        lax.psum(shards[4].astype(jnp.bfloat16), "dp").astype(jnp.float32),
        lax.psum(shards[5].astype(jnp.bfloat16), "dp").astype(jnp.float32),
    )
    return (
        layer_out,
        grad_tokens,
        shards[0],
        shards[1],
        shards[2],
        shards[3],
        shards[4],
        shards[5],
    )


def solution(mesh):
    placed = (
        P(("dp", "fsdp"), None),
        P(("dp", "fsdp")),
        P(("dp", "fsdp")),
        P("fsdp"),
        P("fsdp", None),
        P("fsdp", None),
        P("fsdp"),
        P("fsdp", None),
        P("fsdp", None),
        P(("dp", "fsdp"), None),
    )
    return jax.shard_map(
        body,
        mesh=mesh,
        in_specs=placed,
        out_specs=(
            P(("dp", "fsdp"), None),
            P(("dp", "fsdp"), None),
            P("fsdp"),
            P("fsdp", None),
            P("fsdp", None),
            P("fsdp"),
            P("fsdp", None),
            P("fsdp", None),
        ),
        check_vma=False,
    )
```

profile of v0, /device:TPU:0, one launch (start us, length us, event | category | flops | bytes accessed | tf_op | source)
XLA Modules:
  0.0 1281.2 jit_solution(11775041024302519198)
XLA Ops:
  30.8 61.8 %all-gather.7.cloned.1.call-done = bf16[1024,3072]{1,0:T(8,128)(2,1)} async-done(((bf16[512,3072]{1,0:T(8,128)(2,1)}), bf16[1024,3072]{1,0:T(8,128)(2,1)}) %all-gather.7.cloned.1.call-update) | async-done | bytes 6291472 | tf_op jit(solution)/shard_map/all_gather | solution.py:81
  92.7 9.3 fusion.69
  106.6 6.1 copy.47
  139.6 6.3 collective-permute-done.1
  145.9 6.1 pad_maximum_fusion.4
  152.0 6.8 copy.50
  158.8 73.4 %while.30 = (s32[]{:T(128)}, bf16[2,512,1024]{2,1,0:T(8,128)(2,1)}, f32[2,16,512]{2,1,0:T(8,128)S(1)}, s32[2]{0:T(128)S(1)}, bf16[1152,2048]{0,1:T(8,128)(2,1)},...) while((s32[]{:T(128)}, bf16[2,512,1024]{2,1,0:T(8,128)(2,1)}, ...), condition=%wide.region_5.6_spmd, body=%wide.region_2.5_spmd.sunk | while | flops 1408041472 | bytes 83921080 | solution.py:165
  173.3 6.2 fusion.130
  184.7 8.2 fusion.132
  209.7 6.2 fusion.130
  221.1 8.2 fusion.132
  240.8 21.3 %all-gather.11.cloned.1.call-done = bf16[1024,5248]{1,0:T(8,128)(2,1)} async-done(((bf16[512,5248]{1,0:T(8,128)(2,1)}), bf16[1024,5248]{1,0:T(8,128)(2,1)}) %all-gather.11.cloned.1.call-update) | async-done | bytes 10747920 | tf_op jit(solution)/shard_map/all_gather | solution.py:84
  262.2 20.9 %fusion.75 = f32[1024,5248]{1,0:T(8,128)} fusion(bf16[1024,5248]{1,0:T(8,128)(2,1)} %all-gather.11.cloned.1.call-done, f32[1024,1024]{0,1:T(8,128)} %copy-done.11, f32[1024]{0:T(1024)S(1)} %bitcast.119, f32[1024]{0:T(1024)S(1)} %add_rsqrt_fusion, f32[1024]{0:T(1024)S(1)} %broadcast_multiply_fusion.5), kind=kOutput, calls=%fused_computation.160 | convolution fusion | flops 11010048000 | bytes 36450304 | tf_op jit(solution)/shard_map/dot_general | solution.py:170
  283.1 50.5 %all-gather.13.cloned.1.call-done = bf16[2624,1024]{1,0:T(8,128)(2,1)} async-done(((bf16[1312,1024]{1,0:T(8,128)(2,1)}), bf16[2624,1024]{1,0:T(8,128)(2,1)}) %all-gather.13.cloned.1.call-update) | async-done | bytes 5373968 | tf_op jit(solution)/shard_map/all_gather | solution.py:85
  333.7 36.5 %add_convert_fusion = (bf16[1024,2624]{1,0:T(8,128)(2,1)}, f32[1024,2624]{1,0:T(8,128)}, f32[1024,2624]{1,0:T(8,128)}) fusion(f32[1024,5248]{1,0:T(8,128)} %fusion.75, bf16[1024,1024]{1,0:T(8,128)(2,1)S(1)} %copy-done.18, bf16[2624,1024]{1,0:T(8,128)(2,1)} %all-gather.13.cloned.1.call-done), kind=kOutput, calls=%fused_computation.71 | convolution fusion | flops 5699076096 | bytes 55836672 | tf_op jit(solution)/shard_map/nd,fd->nf/dot_general | solution.py:186
  370.2 19.7 %multiply_convert_fusion.1 = (bf16[1024,2624]{1,0:T(8,128)(2,1)}, bf16[1024,2624]{1,0:T(8,128)(2,1)}) fusion(f32[1024,2624]{1,0:T(8,128)} %get-tuple-element.541, f32[1024,2624]{1,0:T(8,128)} %get-tuple-element.503, f32[1024,5248]{1,0:T(8,128)} %fusion.75), kind=kLoop, calls=%fused_computation.70 | loop fusion | flops 16121856 | bytes 53739520 | tf_op jit(solution)/shard_map/convert.13
  389.9 20.7 %multiply_reduce_fusion.1 = (bf16[1024]{0:T(1024)(128)(2,1)}, f32[1024]{0:T(1024)S(1)}, f32[1024]{0:T(1024)S(1)}, f32[1024,1024]{0,1:T(8,128)}) fusion(f32[1024,1024]{0,1:T(8,128)S(1)} %copy-done.12, f32[1024]{0:T(1024)S(1)} %add_rsqrt_fusion, f32[1024]{0:T(1024)S(1)} %broadcast_multiply_fusion.5, f32[1024]{0:T(1024)S(1)} %bitcast.120, ...), kind=kOutput, calls=%fused_computation.112 | convolution fusion | flops 11035735040 | bytes 29906944 | tf_op jit(solution)/shard_map/nf,df->nd/dot_general | solution.py:190
  420.0 10.1 convolution_convert_fusion.1
  441.8 313.6 %while.31 = (s32[]{:T(128)}, f32[1152,2048]{0,1:T(8,128)}, f32[2,512,1024]{1,0,2:T(2,128)}, s32[2]{0:T(128)S(1)}, bf16[1024,16,64]{0,2,1:T(8,128)(2,1)}, /*index...) while((s32[]{:T(128)}, f32[1152,2048]{0,1:T(8,128)}, ...), condition=%wide.region_12.13_spmd, body=%wide.region_10.12_spmd.sunk | while | flops 3440837120 | bytes 286787264 | solution.py:238
  449.2 12.4 fusion.143
  466.2 16.2 %multiply_reduce_fusion.7 = (f32[16,512]{1,0:T(8,128)S(1)}, f32[16,512,640]{2,1,0:T(8,128)}) fusion(f32[16,512,640]{2,1,0:T(8,128)} %fusion.143, f32[16,512]{1,0:T(8,128)S(1)} %dynamic-slice_bitcast_fusion.2, pred[512,640]{1,0:T(8,128)(4,1)S(1)} %fusion.146, bf16[640,16,64]{0,2,1:T(8,128)(2,1)S(1)} %bitcast.101, ...), kind=kOutput, calls=%fused_computation.30.clone.1 | convolution fusion | flops 697294848 | bytes 44695556 | tf_op jit(solution)/shard_map/while/body/eval_jaxpr/qhd,khd->hqk/dot_general | solution.py:205
  482.4 19.3 %multiply_convert_fusion.7 = bf16[16,512,640]{2,1,0:T(8,128)(2,1)} fusion(f32[16,512,640]{2,1,0:T(8,128)} %get-tuple-element.722, f32[16,512,640]{2,1,0:T(8,128)} %fusion.143, f32[16,512]{1,0:T(8,128)S(1)} %get-tuple-element.723, f32[16,512]{1,0:T(8,128)S(1)} %dynamic-slice_bitcast_fusion.2, pred[512,640]{1,0:T(8,128)(4,1)S(1)} %fusion.146), kind=kLoop, calls=%fused_computation.29.clone.1 | loop fusion | flops 31457280 | bytes 52822016 | tf_op jit(solution)/shard_map/while/body/eval_jaxpr/convert_element_type | solution.py:209
  501.7 8.5 convolution_multiply_fusion.4
  510.3 8.2 fusion.147
  518.5 8.3 maximum_add_fusion.2
  526.7 25.4 %dynamic_update_slice.34 = f32[1152,2048]{0,1:T(8,128)} dynamic-update-slice(f32[1152,2048]{0,1:T(8,128)} %get-tuple-element.791, f32[640,2048]{0,1:T(8,128)} %maximum_add_fusion.2, s32[]{:T(128)S(6)} %select_n.139, s32[]{:T(128)} %constant.244.clone.1..sunk.1) | dynamic-update-slice | bytes 10485764 | tf_op jit(solution)/shard_map/while/body/eval_jaxpr/dynamic_update_slice | solution.py:232
  552.1 7.3 convolution_multiply_fusion.5
  561.6 37.7 %dynamic_update_slice.35 = f32[2,512,1024]{1,0,2:T(2,128)} dynamic-update-slice(f32[2,512,1024]{1,0,2:T(2,128)} %get-tuple-element.792, f32[1,512,1024]{1,0,2:T(1,128)S(1)} %copy.79, s32[]{:T(128)} %get-tuple-element.790, s32[]{:T(128)} %constant.244.clone.1..sunk.1, s32[]{:T(128)} %constant.244.clone.1..sunk.1) | dynamic-update-slice | bytes 4194308 | tf_op jit(solution)/shard_map/while/body/jit(dynamic_update_index_in_dim)/dynamic_update_slice | solution.py:165
  606.3 11.6 fusion.143
  622.5 16.1 %multiply_reduce_fusion.7 = (f32[16,512]{1,0:T(8,128)S(1)}, f32[16,512,640]{2,1,0:T(8,128)}) fusion(f32[16,512,640]{2,1,0:T(8,128)} %fusion.143, f32[16,512]{1,0:T(8,128)S(1)} %dynamic-slice_bitcast_fusion.2, pred[512,640]{1,0:T(8,128)(4,1)S(1)} %fusion.146, bf16[640,16,64]{0,2,1:T(8,128)(2,1)S(1)} %bitcast.101, ...), kind=kOutput, calls=%fused_computation.30.clone.1 | convolution fusion | flops 697294848 | bytes 44695556 | tf_op jit(solution)/shard_map/while/body/eval_jaxpr/qhd,khd->hqk/dot_general | solution.py:205
  638.6 20.1 %multiply_convert_fusion.7 = bf16[16,512,640]{2,1,0:T(8,128)(2,1)} fusion(f32[16,512,640]{2,1,0:T(8,128)} %get-tuple-element.722, f32[16,512,640]{2,1,0:T(8,128)} %fusion.143, f32[16,512]{1,0:T(8,128)S(1)} %get-tuple-element.723, f32[16,512]{1,0:T(8,128)S(1)} %dynamic-slice_bitcast_fusion.2, pred[512,640]{1,0:T(8,128)(4,1)S(1)} %fusion.146), kind=kLoop, calls=%fused_computation.29.clone.1 | loop fusion | flops 31457280 | bytes 52822016 | tf_op jit(solution)/shard_map/while/body/eval_jaxpr/convert_element_type | solution.py:209
  658.7 8.5 convolution_multiply_fusion.4
  667.2 8.2 fusion.147
  675.4 7.8 maximum_add_fusion.2
  683.2 24.6 %dynamic_update_slice.34 = f32[1152,2048]{0,1:T(8,128)} dynamic-update-slice(f32[1152,2048]{0,1:T(8,128)} %get-tuple-element.791, f32[640,2048]{0,1:T(8,128)} %maximum_add_fusion.2, s32[]{:T(128)S(6)} %select_n.139, s32[]{:T(128)} %constant.244.clone.1..sunk.1) | dynamic-update-slice | bytes 10485764 | tf_op jit(solution)/shard_map/while/body/eval_jaxpr/dynamic_update_slice | solution.py:232
  707.8 7.3 convolution_multiply_fusion.5
  717.3 37.7 %dynamic_update_slice.35 = f32[2,512,1024]{1,0,2:T(2,128)} dynamic-update-slice(f32[2,512,1024]{1,0,2:T(2,128)} %get-tuple-element.792, f32[1,512,1024]{1,0,2:T(1,128)S(1)} %copy.79, s32[]{:T(128)} %get-tuple-element.790, s32[]{:T(128)} %constant.244.clone.1..sunk.1, s32[]{:T(128)} %constant.244.clone.1..sunk.1) | dynamic-update-slice | bytes 4194308 | tf_op jit(solution)/shard_map/while/body/jit(dynamic_update_index_in_dim)/dynamic_update_slice | solution.py:165
  768.7 6.6 reshape.570
  803.8 12.1 convolution_convert_fusion.2
  816.5 19.7 %convolution_convert_fusion = bf16[1024,5248]{1,0:T(8,128)(2,1)} fusion(bf16[1024,2624]{1,0:T(8,128)(2,1)} %get-tuple-element.516, bf16[1024,2624]{1,0:T(8,128)(2,1)} %get-tuple-element.502, f32[1024,1024]{0,1:T(8,128)} %copy-done.11, f32[1024]{0:T(1024)S(1)} %bitcast.122, f32[1024]{0:T(1024)S(1)} %copy-done.43, f32[1024]{0:T(1024)S(1)} %copy-done.35), kind=kOutput, calls=%fused_computation.68 | convolution fusion | flops 11036917760 | bytes 25702400 | tf_op jit(solution)/shard_map/nd,nf->df/dot_general | solution.py:189
  836.3 57.5 %reduce-scatter.5.cloned.1.call-done = bf16[512,3072]{1,0:T(8,128)(2,1)} async-done(((bf16[1024,3072]{1,0:T(8,128)(2,1)}), bf16[512,3072]{1,0:T(8,128)(2,1)}) %reduce-scatter.5.cloned.1.call-update) | async-done | bytes 3145744 | tf_op jit(solution)/shard_map/reduce_scatter | solution.py:275
  893.8 127.7 %reduce-scatter.9.cloned.1.call-done = bf16[512,5248]{1,0:T(8,128)(2,1)} async-done(((bf16[1024,5248]{1,0:T(8,128)(2,1)}), bf16[512,5248]{1,0:T(8,128)(2,1)}) %reduce-scatter.9.cloned.1.call-update) | async-done | bytes 5373968 | tf_op jit(solution)/shard_map/reduce_scatter | solution.py:284
  1023.4 11.4 add_convert_fusion.1
  1038.7 12.8 %fusion.63 = (bf16[1024]{0:T(1024)(128)(2,1)S(1)}, f32[1024]{0:T(1024)S(1)}, f32[1024]{0:T(1024)S(1)}, f32[1024,1024]{0,1:T(8,128)}) fusion(bf16[1024,1024]{0,1:T(8,128)(2,1)S(1)} %copy-done.5, f32[1024]{0:T(1024)S(1)} %copy-done.37, f32[1024]{0:T(1024)S(1)} %copy-done.33, f32[1024]{0:T(1024)S(1)} %bitcast.117, ...), kind=kOutput, calls=%fused_computation.108 | convolution fusion | flops 6470759424 | bytes 18896896 | tf_op jit(solution)/shard_map/nf,df->nd/dot_general | solution.py:265
  1056.6 34.5 %all-reduce.2 = (bf16[512]{0:T(512)(128)(2,1)S(1)}, bf16[512]{0:T(512)(128)(2,1)S(1)}) all-reduce(bf16[512]{0:T(512)(128)(2,1)S(1)} %dynamic-slice.17, bf16[512]{0:T(512)(128)(2,1)S(1)} %dynamic-slice.19), channel_id=1, replica_groups=mesh['dp'=16,'fsdp'=2] {'dp'}, use_global_device_ids=true, to_apply=%region_17.18 | all-reduce | flops 1024 | bytes 4096 | tf_op jit(solution)/shard_map/psum | solution.py:292
  1092.3 6.9 fusion.62
  1104.5 154.2 %all-reduce.7.cloned.1.call-done = (bf16[512,3072]{1,0:T(8,128)(2,1)}, bf16[512,1024]{1,0:T(8,128)(2,1)}, bf16[512,5248]{1,0:T(8,128)(2,1)}, bf16[1312,1024]{1,0:T(8,128)(2,1)}) async-done(((bf16[512,3072]{1,0:T(8,128)(2,1)}, bf16[512,1024]{1,0:T(8,128)(2,1)}, bf16[512,5248]{1,0:T(8,128)(2,1)}, bf16[1312,1024]{1,0:T(8,128)(2,1)}), (bf16[512,3072]{1,0:T(8,128)(2,1)}, bf16[512,1024]{1,0:T(8,128)(2,1)}, ...) | async-done | bytes 12255248 | tf_op jit(solution)/shard_map/psum | solution.py:293
  1258.7 7.6 convert_element_type.143
  (284 shorter events, 210.3 us)
Async XLA Ops:
  7.2 85.5 %all-gather.7.cloned.1.call-start = ((), (), s32[]{:S(2)}) async-start(), calls=%async_computation.4 | async-start | bytes 9437184 | tf_op jit(solution)/shard_map/all_gather | solution.py:81
  7.9 224.3 %all-gather.9.cloned.1.call-start = ((), (), s32[]{:S(2)}) async-start(), calls=%async_computation.5 | async-start | bytes 3145728 | tf_op jit(solution)/shard_map/all_gather | solution.py:82
  8.6 253.5 %all-gather.11.cloned.1.call-start = ((), (), s32[]{:S(2)}) async-start(), calls=%async_computation.6 | async-start | bytes 16121856 | tf_op jit(solution)/shard_map/all_gather | solution.py:84
  9.4 324.3 %all-gather.13.cloned.1.call-start = ((), (), s32[]{:S(2)}) async-start(), calls=%async_computation.7 | async-start | bytes 8060928 | tf_op jit(solution)/shard_map/all_gather | solution.py:85
  10.0 826.3 %reduce-scatter.7.cloned.1.call-start = ((), (), s32[]{:S(2)}) async-start(), calls=%async_computation.9 | async-start | bytes 3145728 | tf_op jit(solution)/shard_map/reduce_scatter | solution.py:278
  10.1 9.2 copy-start.28
  10.1 9.2 copy-start.30
  10.1 10.5 copy-start.46
  13.0 79.7 %copy-start.4 = (bf16[1024,1024]{0,1:T(8,128)(2,1)}, bf16[1024,1024]{0,1:T(8,128)(2,1)S(1)}, u32[]{:S(2)}) copy-start(bf16[1024,1024]{0,1:T(8,128)(2,1)S(1)} %copy.46) | copy-start | bytes 6291460
  13.4 88.6 %copy-start.32 = (f32[1024]{0:T(1024)}, f32[1024]{0:T(1024)S(1)}, u32[]{:S(2)}) copy-start(f32[1024]{0:T(1024)S(1)} %broadcast_multiply_fusion.6) | copy-start | bytes 12292
  14.0 88.0 %copy-start.36 = (f32[1024]{0:T(1024)}, f32[1024]{0:T(1024)S(1)}, u32[]{:S(2)}) copy-start(f32[1024]{0:T(1024)S(1)} %add_rsqrt_fusion.1) | copy-start | bytes 12292
  19.3 82.7 %copy-start.38 = (f32[2,1,512]{2,1,0:T(1,128)}, f32[2,1,512]{2,1,0:T(1,128)S(1)}, u32[]{:S(2)}) copy-start(f32[2,1,512]{2,1,0:T(1,128)S(1)} %convert_element_type.146) | copy-start | bytes 12292
  30.8 87.2 %copy-start.21 = (f32[1024,32]{0,1:T(8,128)}, f32[1024,32]{0,1:T(8,128)S(1)}, u32[]{:S(2)}) copy-start(f32[1024,32]{0,1:T(8,128)S(1)} %get-tuple-element.538) | copy-start | bytes 393220
  106.6 22.8 %copy-start.7 = (bf16[1024,1024]{1,0:T(8,128)(2,1)}, bf16[1024,1024]{1,0:T(8,128)(2,1)S(1)}, u32[]{:S(2)}) copy-start(bf16[1024,1024]{1,0:T(8,128)(2,1)S(1)} %slice.208) | copy-start | bytes 6291460
  129.3 16.5 %copy-start.9 = (bf16[1024,1024]{1,0:T(8,128)(2,1)S(1)}, bf16[1024,1024]{1,0:T(8,128)(2,1)}, u32[]{:S(2)}) copy-start(bf16[1024,1024]{1,0:T(8,128)(2,1)} %copy.48) | copy-start | bytes 6291460
  130.5 15.4 %copy-start.8 = (bf16[1024,1024]{1,0:T(8,128)(2,1)S(1)}, bf16[1024,1024]{1,0:T(8,128)(2,1)}, u32[]{:S(2)}) copy-start(bf16[1024,1024]{1,0:T(8,128)(2,1)} %copy-done.7) | copy-start | bytes 6291460
  130.5 9.1 collective-permute-start
  132.9 13.0 %collective-permute-start.1 = (bf16[64,2048]{1,0:T(8,128)(2,1)S(1)}, bf16[64,2048]{1,0:T(8,128)(2,1)S(1)}, u32[]{:S(2)}, u32[]{:S(2)}) collective-permute-start(bf16[64,2048]{1,0:T(8,128)(2,1)S(1)} %get-tuple-element.531), channel_id=1, source_target_pairs={{1,0},{2,1},{3,2},{4,3},{5,4},{6,5},{7,6},{8,7},{9,8},{10,9},{11,1... | collective-permute-start | bytes 786440 | tf_op jit(solution)/shard_map/ppermute | solution.py:23
  232.2 6.1 copy-start.1
  238.3 23.8 %copy-start.40 = (f32[2,1,512]{2,1,0:T(1,128)S(1)}, f32[2,1,512]{2,1,0:T(1,128)}, u32[]{:S(2)}) copy-start(f32[2,1,512]{2,1,0:T(1,128)} %convert_element_type.147) | copy-start | bytes 12292
  238.4 172.3 %copy-start.34 = (f32[1024]{0:T(1024)}, f32[1024]{0:T(1024)S(1)}, u32[]{:S(2)}) copy-start(f32[1024]{0:T(1024)S(1)} %broadcast_multiply_fusion.5) | copy-start | bytes 12292
  240.8 169.8 %copy-start.42 = (f32[1024]{0:T(1024)}, f32[1024]{0:T(1024)S(1)}, u32[]{:S(2)}) copy-start(f32[1024]{0:T(1024)S(1)} %add_rsqrt_fusion) | copy-start | bytes 12292
  262.2 71.5 %copy-start.18 = (bf16[1024,1024]{1,0:T(8,128)(2,1)S(1)}, bf16[1024,1024]{1,0:T(8,128)(2,1)}, u32[]{:S(2)}) copy-start(bf16[1024,1024]{1,0:T(8,128)(2,1)} %param.27) | copy-start | bytes 6291460
  370.2 19.7 %copy-start.12 = (f32[1024,1024]{0,1:T(8,128)S(1)}, f32[1024,1024]{0,1:T(8,128)}, u32[]{:S(2)}) copy-start(f32[1024,1024]{0,1:T(8,128)} %copy-done.11) | copy-start | bytes 12582916
  389.9 20.7 %copy-start.14 = (bf16[1024,1024]{0,1:T(8,128)(2,1)S(1)}, bf16[1024,1024]{0,1:T(8,128)(2,1)}, u32[]{:S(2)}) copy-start(bf16[1024,1024]{0,1:T(8,128)(2,1)} %copy.53) | copy-start | bytes 6291460
  420.0 416.3 %reduce-scatter.11.cloned.1.call-start = ((), (), s32[]{:S(2)}) async-start(), calls=%async_computation.11 | async-start | bytes 8060928 | tf_op jit(solution)/shard_map/reduce_scatter | solution.py:287
  430.2 463.6 %reduce-scatter.5.cloned.1.call-start = ((), (), s32[]{:S(2)}) async-start(), calls=%async_computation.8 | async-start | bytes 9437184 | tf_op jit(solution)/shard_map/reduce_scatter | solution.py:275
  466.1 16.2 %copy-start.3 = (pred[512,640]{1,0:T(8,128)(4,1)}, pred[512,640]{1,0:T(8,128)(4,1)S(1)}, u32[]{:S(2)}) copy-start(pred[512,640]{1,0:T(8,128)(4,1)S(1)} %fusion.146) | copy-start | bytes 983044 | tf_op jit(solution)/shard_map/while
  482.3 19.4 %copy-start.2 = (bf16[1024,16,64]{0,2,1:T(8,128)(2,1)S(1)}, bf16[1024,16,64]{0,2,1:T(8,128)(2,1)}, u32[]{:S(2)}) copy-start(bf16[1024,16,64]{0,2,1:T(8,128)(2,1)} %get-tuple-element.812) | copy-start | bytes 6291460 | tf_op jit(solution)/shard_map/while
  482.3 27.9 %slice-start = ((s8[20971520]{0:T(1024)(128)(4,1)}), s8[4194304]{0:T(1024)(128)(4,1)S(1)}, s32[]{:S(2)}) async-start(s8[20971520]{0:T(1024)(128)(4,1)} %bitcast.95), calls=%async_computation.13 | async-start | bytes 8388608 | tf_op jit(solution)/shard_map/while
  482.3 27.9 %slice-start.1 = ((s8[20971520]{0:T(1024)(128)(4,1)}), s8[4194304]{0:T(1024)(128)(4,1)S(1)}, s32[]{:S(2)}) async-start(s8[20971520]{0:T(1024)(128)(4,1)} %bitcast.95), calls=%async_computation.14 | async-start | bytes 8388608 | tf_op jit(solution)/shard_map/while
  482.3 27.9 %slice-start.2 = ((s8[20971520]{0:T(1024)(128)(4,1)}), s8[4194304]{0:T(1024)(128)(4,1)S(1)}, s32[]{:S(2)}) async-start(s8[20971520]{0:T(1024)(128)(4,1)} %bitcast.95), calls=%async_computation.15 | async-start | bytes 8388608 | tf_op jit(solution)/shard_map/while
  482.3 27.9 %slice-start.3 = ((s8[20971520]{0:T(1024)(128)(4,1)}), s8[4194304]{0:T(1024)(128)(4,1)S(1)}, s32[]{:S(2)}) async-start(s8[20971520]{0:T(1024)(128)(4,1)} %bitcast.95), calls=%async_computation.16 | async-start | bytes 8388608 | tf_op jit(solution)/shard_map/while
  501.7 8.5 slice-start.4
  622.4 16.2 %copy-start.3 = (pred[512,640]{1,0:T(8,128)(4,1)}, pred[512,640]{1,0:T(8,128)(4,1)S(1)}, u32[]{:S(2)}) copy-start(pred[512,640]{1,0:T(8,128)(4,1)S(1)} %fusion.146) | copy-start | bytes 983044 | tf_op jit(solution)/shard_map/while
  638.6 20.1 %copy-start.2 = (bf16[1024,16,64]{0,2,1:T(8,128)(2,1)S(1)}, bf16[1024,16,64]{0,2,1:T(8,128)(2,1)}, u32[]{:S(2)}) copy-start(bf16[1024,16,64]{0,2,1:T(8,128)(2,1)} %get-tuple-element.812) | copy-start | bytes 6291460 | tf_op jit(solution)/shard_map/while
  638.6 28.6 %slice-start = ((s8[20971520]{0:T(1024)(128)(4,1)}), s8[4194304]{0:T(1024)(128)(4,1)S(1)}, s32[]{:S(2)}) async-start(s8[20971520]{0:T(1024)(128)(4,1)} %bitcast.95), calls=%async_computation.13 | async-start | bytes 8388608 | tf_op jit(solution)/shard_map/while
  638.6 28.6 %slice-start.1 = ((s8[20971520]{0:T(1024)(128)(4,1)}), s8[4194304]{0:T(1024)(128)(4,1)S(1)}, s32[]{:S(2)}) async-start(s8[20971520]{0:T(1024)(128)(4,1)} %bitcast.95), calls=%async_computation.14 | async-start | bytes 8388608 | tf_op jit(solution)/shard_map/while
  638.6 28.6 %slice-start.2 = ((s8[20971520]{0:T(1024)(128)(4,1)}), s8[4194304]{0:T(1024)(128)(4,1)S(1)}, s32[]{:S(2)}) async-start(s8[20971520]{0:T(1024)(128)(4,1)} %bitcast.95), calls=%async_computation.15 | async-start | bytes 8388608 | tf_op jit(solution)/shard_map/while
  638.6 28.6 %slice-start.3 = ((s8[20971520]{0:T(1024)(128)(4,1)}), s8[4194304]{0:T(1024)(128)(4,1)S(1)}, s32[]{:S(2)}) async-start(s8[20971520]{0:T(1024)(128)(4,1)} %bitcast.95), calls=%async_computation.16 | async-start | bytes 8388608 | tf_op jit(solution)/shard_map/while
  658.7 8.5 slice-start.4
  755.4 6.4 copy-start
  760.0 15.3 %collective-permute-start.2 = (bf16[64,2048]{0,1:T(8,128)(2,1)S(1)}, bf16[64,2048]{0,1:T(8,128)(2,1)S(1)}, u32[]{:S(2)}, u32[]{:S(2)}) collective-permute-start(bf16[64,2048]{0,1:T(8,128)(2,1)S(1)} %get-tuple-element.521), channel_id=1, source_target_pairs={{0,1},{1,2},{2,3},{3,4},{4,5},{5,6},{6,7},{7,8},{8,9},{9,10},{10,1... | collective-permute-start | bytes 786440 | tf_op jit(solution)/shard_map/ppermute | solution.py:31
  767.4 18.9 %collective-permute-start.3 = (bf16[64,2048]{0,1:T(8,128)(2,1)S(1)}, bf16[64,2048]{0,1:T(8,128)(2,1)S(1)}, u32[]{:S(2)}, u32[]{:S(2)}) collective-permute-start(bf16[64,2048]{0,1:T(8,128)(2,1)S(1)} %get-tuple-element.520), channel_id=1, source_target_pairs={{1,0},{2,1},{3,2},{4,3},{5,4},{6,5},{7,6},{8,7},{9,8},{10,9},{11,1... | collective-permute-start | bytes 786440 | tf_op jit(solution)/shard_map/ppermute | solution.py:31
  815.9 205.6 %reduce-scatter.9.cloned.1.call-start = ((), (), s32[]{:S(2)}) async-start(), calls=%async_computation.10 | async-start | bytes 16121856 | tf_op jit(solution)/shard_map/reduce_scatter | solution.py:284
  836.2 422.5 %all-reduce.7.cloned.1.call-start = ((), (), s32[]{:S(2)}) async-start(), calls=%async_computation.12 | async-start | bytes 24510464 | tf_op jit(solution)/shard_map/psum | solution.py:293
  1038.7 12.8 %copy-start.44 = (bf16[1024]{0:T(1024)(128)(2,1)S(1)}, bf16[1024]{0:T(1024)(128)(2,1)}, u32[]{:S(2)}) copy-start(bf16[1024]{0:T(1024)(128)(2,1)} %get-tuple-element.436) | copy-start | bytes 6148
  1258.7 7.6 copy-start.16
  (34 other events, 116.3 us)
Sparse Core Ops, SparseCore 0:
  9.5 83.0 all-gather.6
  94.2 33.1 all-gather.8
  128.9 133.2 all-gather.10
  263.6 70.0 all-gather.12
  420.1 31.8 reduce-scatter.6
  454.8 67.1 reduce-scatter.10
  816.0 77.7 reduce-scatter.4
  896.8 124.6 reduce-scatter.8
  1026.9 231.7 all-reduce.6
where the time goes:
time: 1300 us; the launch traced here: 1280 us
  waiting for transfers between devices  491 us (38%)
  matrix products  302 us (23%)
  local copies, waits for them, and re-layouts  242 us (19%)
  other arithmetic  160 us (12%)
  blocking collectives  49 us (4%)
  between operations  15.4 us (1%)
  loops' own time  14.3 us (1%)
    psum x1, waiting for transfers between devices, body(): lax.psum(shards[1].astype(jnp.bfloat16), 'dp').astype(jnp.float32)  154 us
    reduce_scatter x1, waiting for transfers between devices, body(): lax.psum_scatter(gradients[4].astype(jnp.bfloat16), 'fsdp', scatter_dimen...  128 us
    dynamic_update_slice x8, local copies, waits for them, and re-layouts, body(): attended, log_totals = lax.map(block_forward, block_rows)  84.9 us
    all_gather x1, waiting for transfers between devices, body(): lax.all_gather(weights[1], 'fsdp', axis=0, tiled=True)  61.8 us
    reduce_scatter x1, waiting for transfers between devices, body(): lax.psum_scatter(gradients[1].astype(jnp.bfloat16), 'fsdp', scatter_dimen...  57.5 us
    all_gather x1, waiting for transfers between devices, body(): lax.all_gather(weights[5], 'fsdp', axis=0, tiled=True)  50.5 us
    dynamic_update_slice x2, local copies, waits for them, and re-layouts, block_backward(): lax.dynamic_update_slice_in_dim(accumulated, current + block_grad, first_...  50 us
    convert_element_type x2, other arithmetic, block_backward(): grad_scores = (probs * (grad_probs - centre)).astype(jnp.bfloat16)  39.4 us
  transfers between devices with their start and end apart: 13, of which 9 were waited for; matrix products, arithmetic and copies ran while one was open for 47% of the time, Pallas kernels for 0%

commit v1 on v0

v1 whole, which is shorter than its diff:
```python
import jax
import jax.numpy as jnp
from jax import lax
from jax.experimental import pallas as pl
from jax.experimental.pallas import tpu as pltpu
from jax.sharding import PartitionSpec as P

HEADS = 16
HALF = 64
QROWS = 128
KSPAN = QROWS + 2 * HALF
LANES = 128

EPSILON = 1e-05
MASKED = -1e30
STREAM = ("dp", "fsdp")
NT = (((1,), (1,)), ((), ()))
TN = (((0,), (0,)), ((), ()))
F32 = jnp.float32
BF16 = jnp.bfloat16


def passed_along(x, axis, by):
    devices = lax.axis_size(axis)
    pairs = [(i, i + by) for i in range(devices) if 0 <= i + by < devices]
    return lax.ppermute(x, axis, pairs)


def norm_forward(values, gain):
    average = jnp.mean(values, axis=-1, keepdims=True)
    centred = values - average
    inverse = lax.rsqrt(jnp.mean(centred * centred, axis=-1, keepdims=True) + EPSILON)
    scaled = centred * inverse
    return (scaled * gain, scaled, inverse)


def norm_backward(incoming, gain, scaled, inverse):
    weighted = incoming * gain
    inner = weighted - jnp.mean(weighted, axis=-1, keepdims=True)
    inner = inner - scaled * jnp.mean(weighted * scaled, axis=-1, keepdims=True)
    return (inner * inverse, jnp.sum(incoming * scaled, axis=0))


def exact_gelu(values):
    return jax.nn.gelu(values, approximate=False)


def params(limit=48):
    return pltpu.CompilerParams(vmem_limit_bytes=limit * 1024 * 1024)


def turned(x, cosine, sine):
    lane = lax.broadcasted_iota(jnp.int32, x.shape, 1)
    swapped = jnp.where(
        lane % 64 < 32, pltpu.roll(x, LANES - 32, 1), pltpu.roll(x, 32, 1)
    )
    return x * cosine + swapped * sine


def qkv_kernel(act_ref, w_ref, cos_ref, sin_ref, out_ref):
    step = pl.program_id(0)
    width = out_ref.shape[1]
    per_part = pl.num_programs(0) // 3
    rows = act_ref.shape[0]
    chunk = 256

    def product(first):
        return jnp.dot(act_ref[first : first + chunk, :], w_ref[...], preferred_element_type=F32)

    @pl.when(step < 2 * per_part)
    def _():
        scale = jnp.where(step < per_part, 0.125, 1.0).astype(F32)
        for first in range(0, rows, chunk):
            x = product(first)
            cosine = cos_ref[first : first + chunk, :]
            sine = sin_ref[first : first + chunk, :]
            for lo in range(0, width, LANES):
                part = turned(x[:, lo : lo + LANES], cosine, sine) * scale
                out_ref[first : first + chunk, lo : lo + LANES] = part.astype(BF16)

    @pl.when(step >= 2 * per_part)
    def _():
        for first in range(0, rows, chunk):
            out_ref[first : first + chunk, :] = product(first).astype(BF16)


def project_qkv(act, w, cosine, sine):
    rows, depth = act.shape
    total = w.shape[1]
    width = 256
    return pl.pallas_call(
        qkv_kernel,
        grid=(total // width,),
        in_specs=[
            pl.BlockSpec((rows, depth), lambda j: (0, 0)),
            pl.BlockSpec((depth, width), lambda j: (0, j)),
            pl.BlockSpec((rows, LANES), lambda j: (0, 0)),
            pl.BlockSpec((rows, LANES), lambda j: (0, 0)),
        ],
        out_specs=pl.BlockSpec((rows, width), lambda j: (0, j)),
        out_shape=jax.ShapeDtypeStruct((rows, total), BF16),
        compiler_params=params(),
        cost_estimate=pl.CostEstimate(
            flops=2 * rows * depth * total, bytes_accessed=2 * (rows * depth + depth * total + rows * total), transcendentals=0
        ),
    )(act, w, cosine, sine)


def head_masks():
    first = lax.broadcasted_iota(jnp.int32, (QROWS, LANES), 1) < 64
    one = jnp.where(first, 1.0, 0.0).astype(BF16)
    two = jnp.where(first, 0.0, 1.0).astype(BF16)
    return first, one, two


def attend_kernel(q_ref, k_ref, v_ref, lk_ref, lv_ref, hk_ref, hv_ref, bias_ref, out_ref, lse_ref):
    keys = jnp.concatenate([lk_ref[...], k_ref[...], hk_ref[...]], axis=0)
    values = jnp.concatenate([lv_ref[...], v_ref[...], hv_ref[...]], axis=0)
    first, one, two = head_masks()
    for b in range(q_ref.shape[0] // QROWS):
        at = b * QROWS
        q = q_ref[at : at + QROWS, :]
        pair = jnp.concatenate([q * one, q * two], axis=0)
        bias = bias_ref[b]
        scores = lax.dot_general(keys[at : at + KSPAN], pair, NT, preferred_element_type=F32)
        scores = scores + jnp.concatenate([bias, bias], axis=1)
        highest = jnp.max(scores, axis=0, keepdims=True)
        expo = jnp.exp(scores - highest)
        totals = jnp.sum(expo, axis=0, keepdims=True)
        probs = (expo * (1.0 / totals)).astype(BF16)
        mixed = lax.dot_general(probs, values[at : at + KSPAN], TN, preferred_element_type=F32)
        out_ref[at : at + QROWS, :] = jnp.where(first, mixed[:QROWS], mixed[QROWS:]).astype(BF16)
        lse_ref[b : b + 1, :] = highest + jnp.log(totals)


def halo_specs(pairs):
    return [
        pl.BlockSpec((HALF, LANES), lambda j: (0, j)),
        pl.BlockSpec((HALF, LANES), lambda j, p=pairs: (0, p + j)),
    ]


def attention(qkv, low, high, bias):
    rows = qkv.shape[0]
    width = qkv.shape[1] // 3
    pairs = width // LANES
    blocks = rows // QROWS
    column = lambda by: pl.BlockSpec((rows, LANES), lambda j, by=by: (0, by + j))
    return pl.pallas_call(
        attend_kernel,
        grid=(pairs,),
        in_specs=[column(0), column(pairs), column(2 * pairs)]
        + halo_specs(pairs)
        + halo_specs(pairs)
        + [pl.BlockSpec((blocks, KSPAN, QROWS), lambda j: (0, 0, 0))],
        out_specs=[
            pl.BlockSpec((rows, LANES), lambda j: (0, j)),
            pl.BlockSpec((None, blocks, 2 * QROWS), lambda j: (j, 0, 0)),
        ],
        out_shape=[
            jax.ShapeDtypeStruct((rows, width), BF16),
            jax.ShapeDtypeStruct((pairs, blocks, 2 * QROWS), F32),
        ],
        compiler_params=params(),
        cost_estimate=pl.CostEstimate(
            flops=16 * rows * KSPAN * width, bytes_accessed=8 * rows * width, transcendentals=rows * KSPAN * 16
        ),
    )(qkv, qkv, qkv, low, low, high, high, bias)


def attend_back_kernel(
    q_ref, k_ref, v_ref, lk_ref, lv_ref, hk_ref, hv_ref, bias_ref, do_ref, lse_ref, cos_ref, sin_ref,
    dq_ref, dk_ref, dv_ref, dlk_ref, dlv_ref, dhk_ref, dhv_ref,
):
    keys = jnp.concatenate([lk_ref[...], k_ref[...], hk_ref[...]], axis=0)
    values = jnp.concatenate([lv_ref[...], v_ref[...], hv_ref[...]], axis=0)
    first, one, two = head_masks()
    blocks = q_ref.shape[0] // QROWS
    carry_k = carry_v = None
    for b in range(blocks):
        at = b * QROWS
        q = q_ref[at : at + QROWS, :]
        pair = jnp.concatenate([q * one, q * two], axis=0)
        do = do_ref[at : at + QROWS, :]
        do_pair = jnp.concatenate([do * one, do * two], axis=0)
        key = keys[at : at + KSPAN]
        bias = bias_ref[b]
        scores = lax.dot_general(key, pair, NT, preferred_element_type=F32)
        scores = scores + jnp.concatenate([bias, bias], axis=1)
        probs = jnp.exp(scores - lse_ref[b : b + 1, :])
        dp = lax.dot_general(values[at : at + KSPAN], do_pair, NT, preferred_element_type=F32)
        centre = jnp.sum(probs * dp, axis=0, keepdims=True)
        ds = (probs * (dp - centre)).astype(BF16)
        dk = jnp.dot(ds, pair, preferred_element_type=F32)
        dv = jnp.dot(probs.astype(BF16), do_pair, preferred_element_type=F32)
        dq = lax.dot_general(ds, key, TN, preferred_element_type=F32)
        dq = jnp.where(first, dq[:QROWS], dq[QROWS:]) * 0.125
        dq_ref[at : at + QROWS, :] = turned(
            dq, cos_ref[at : at + QROWS, :], -sin_ref[at : at + QROWS, :]
        ).astype(BF16)
        head_k, head_v = dk[:QROWS], dv[:QROWS]
        if b == 0:
            dlk_ref[...] = head_k[:HALF].astype(BF16)
            dlv_ref[...] = head_v[:HALF].astype(BF16)
            dk_ref[:HALF, :] = head_k[HALF:]
            dv_ref[:HALF, :] = head_v[HALF:]
        else:
            dk_ref[at - HALF : at + HALF, :] = carry_k + head_k
            dv_ref[at - HALF : at + HALF, :] = carry_v + head_v
        carry_k, carry_v = dk[QROWS:], dv[QROWS:]
    end = blocks * QROWS
    dk_ref[end - HALF :, :] = carry_k[:HALF]
    dv_ref[end - HALF :, :] = carry_v[:HALF]
    dhk_ref[...] = carry_k[HALF:].astype(BF16)
    dhv_ref[...] = carry_v[HALF:].astype(BF16)


def attention_back(qkv, low, high, bias, grad_out, lse, cosine, sine):
    rows = qkv.shape[0]
    width = qkv.shape[1] // 3
    pairs = width // LANES
    blocks = rows // QROWS
    column = lambda by: pl.BlockSpec((rows, LANES), lambda j, by=by: (0, by + j))
    edge = pl.BlockSpec((HALF, LANES), lambda j: (0, j))
    table = pl.BlockSpec((rows, LANES), lambda j: (0, 0))
    return pl.pallas_call(
        attend_back_kernel,
        grid=(pairs,),
        in_specs=[column(0), column(pairs), column(2 * pairs)]
        + halo_specs(pairs)
        + halo_specs(pairs)
        + [
            pl.BlockSpec((blocks, KSPAN, QROWS), lambda j: (0, 0, 0)),
            column(0),
            pl.BlockSpec((None, blocks, 2 * QROWS), lambda j: (j, 0, 0)),
            table,
            table,
        ],
        out_specs=[column(0)] * 3 + [edge] * 4,
        out_shape=[jax.ShapeDtypeStruct((rows, width), BF16)]
        + [jax.ShapeDtypeStruct((rows, width), F32)] * 2
        + [jax.ShapeDtypeStruct((HALF, width), BF16)] * 4,
        compiler_params=params(),
        cost_estimate=pl.CostEstimate(
            flops=40 * rows * KSPAN * width, bytes_accessed=20 * rows * width, transcendentals=rows * KSPAN * 16
        ),
    )(qkv, qkv, qkv, low, low, high, high, bias, grad_out, lse, cosine, sine)


def join_kernel(dq_ref, dk_ref, dv_ref, lo_ref, hi_ref, cos_ref, sin_ref, out_ref):
    step = pl.program_id(0)
    per_part = pl.num_programs(0) // 3
    rows = out_ref.shape[0]

    def with_edges(ref):
        return jnp.concatenate(
            [
                ref[:HALF, :] + lo_ref[...].astype(F32),
                ref[HALF : rows - HALF, :],
                ref[rows - HALF :, :] + hi_ref[...].astype(F32),
            ],
            axis=0,
        )

    @pl.when(step < per_part)
    def _():
        out_ref[...] = dq_ref[...]

    @pl.when((step >= per_part) & (step < 2 * per_part))
    def _():
        out_ref[...] = turned(with_edges(dk_ref), cos_ref[...], -sin_ref[...]).astype(BF16)

    @pl.when(step >= 2 * per_part)
    def _():
        out_ref[...] = with_edges(dv_ref).astype(BF16)


def join_grads(dq, dk, dv, from_below, from_above, cosine, sine):
    rows, width = dq.shape
    pairs = width // LANES
    part = lambda by: pl.BlockSpec(
        (rows, LANES), lambda j, by=by: (0, jnp.clip(j - by, 0, pairs - 1))
    )
    edge = pl.BlockSpec((HALF, LANES), lambda j: (0, jnp.maximum(j - pairs, 0)))
    table = pl.BlockSpec((rows, LANES), lambda j: (0, 0))
    return pl.pallas_call(
        join_kernel,
        grid=(3 * pairs,),
        in_specs=[part(0), part(pairs), part(2 * pairs), edge, edge, table, table],
        out_specs=pl.BlockSpec((rows, LANES), lambda j: (0, j)),
        out_shape=jax.ShapeDtypeStruct((rows, 3 * width), BF16),
        compiler_params=params(),
        cost_estimate=pl.CostEstimate(flops=8 * rows * width, bytes_accessed=16 * rows * width, transcendentals=0),
    )(dq, dk, dv, from_below, from_above, cosine, sine)


def visible_bias(segment_ids, positions):
    rows = segment_ids.shape[0]
    blocks = rows // QROWS
    rank = lax.axis_index(STREAM)
    stream_len = rows * lax.axis_size(STREAM)
    edge = jnp.full((HALF,), -1, jnp.int32)
    seg_padded = jnp.concatenate([edge, segment_ids, edge])
    seg_key = jnp.stack([seg_padded[b * QROWS : b * QROWS + KSPAN] for b in range(blocks)])
    seg_key = seg_key[:, :, None]
    seg_query = segment_ids.reshape(blocks, 1, QROWS)
    pos_query = positions.reshape(blocks, 1, QROWS)
    shape = (blocks, KSPAN, QROWS)
    base = lax.broadcasted_iota(jnp.int32, shape, 0) * QROWS
    query_index = base + lax.broadcasted_iota(jnp.int32, shape, 2)
    key_index = base + lax.broadcasted_iota(jnp.int32, shape, 1) - HALF
    nearby = jnp.abs(query_index - key_index) <= HALF
    global_key = rank * rows + key_index
    inside = (global_key >= 0) & (global_key < stream_len)
    earlier_doc = pos_query >= query_index - key_index
    later_doc = seg_query == segment_ids[rows - 1]
    joined = jnp.where(
        key_index < 0, earlier_doc, jnp.where(key_index >= rows, later_doc, seg_query == seg_key)
    )
    return jnp.where(nearby & inside & joined, 0.0, MASKED).astype(F32)


def quads():
    depth, wide = lax.axis_size("dp"), lax.axis_size("fsdp")
    return [
        [(2 * m + c) * wide + f for f in range(wide) for c in range(2)] for m in range(depth // 2)
    ]


def chips():
    return [[2 * m, 2 * m + 1] for m in range(lax.axis_size("dp") // 2)]


def same_core():
    return [[2 * m + c for m in range(lax.axis_size("dp") // 2)] for c in range(2)]


def gathered(shard):
    half = shard.shape[0] // 2
    mine = lax.dynamic_slice_in_dim(shard, (lax.axis_index("dp") % 2) * half, half, 0)
    return lax.all_gather(mine, STREAM, axis=0, tiled=True, axis_index_groups=quads())


def summed(grad):
    part = lax.psum_scatter(
        grad, STREAM, scatter_dimension=0, tiled=True, axis_index_groups=quads()
    )
    part = lax.psum(part, "dp", axis_index_groups=same_core())
    whole = lax.all_gather(part, "dp", axis=0, tiled=True, axis_index_groups=chips())
    return whole.astype(F32)


def body(
    tokens,
    segment_ids,
    positions,
    attn_gain,
    qkv_weight,
    attn_out_weight,
    mlp_gain,
    mlp_in_weight,
    mlp_out_weight,
    out_cotangent,
):
    w_qkv = gathered(qkv_weight)
    gain_one = lax.all_gather(attn_gain, "fsdp", axis=0, tiled=True)
    gain_two = lax.all_gather(mlp_gain, "fsdp", axis=0, tiled=True)
    w_attn = gathered(attn_out_weight)
    w_in = gathered(mlp_in_weight)
    w_out = gathered(mlp_out_weight)
    model_width = tokens.shape[1]
    head_dim = model_width // HEADS
    hidden = w_in.shape[1] // 2

    inputs_f = tokens.astype(F32)
    gain_one = gain_one.astype(F32)
    gain_two = gain_two.astype(F32)
    normed_one, scaled_one, inverse_one = norm_forward(inputs_f, gain_one)
    act_one = normed_one.astype(BF16)
    frequency = jnp.power(10000.0, -jnp.arange(0, head_dim, 2, dtype=F32) / head_dim)
    angles = positions.astype(F32)[:, None] * frequency[None, :]
    cosine = jnp.cos(angles)
    sine = jnp.sin(angles)
    cosine = jnp.concatenate([cosine, cosine, cosine, cosine], axis=1)
    sine = jnp.concatenate([-sine, sine, -sine, sine], axis=1)
    bias = visible_bias(segment_ids, positions)

    qkv = project_qkv(act_one, w_qkv, cosine, sine)
    low = passed_along(qkv[-HALF:, model_width:], STREAM, 1)
    high = passed_along(qkv[:HALF, model_width:], STREAM, -1)
    attended, lse = attention(qkv, low, high, bias)

    resid = inputs_f + jnp.dot(attended, w_attn, preferred_element_type=F32)
    normed_two, scaled_two, inverse_two = norm_forward(resid, gain_two)
    act_two = normed_two.astype(BF16)
    projected = jnp.dot(act_two, w_in, preferred_element_type=F32)
    gating = projected[:, hidden:]
    activated, gelu_pullback = jax.vjp(exact_gelu, projected[:, :hidden])
    product = (activated * gating).astype(BF16)
    grad_wout = jnp.einsum("nf,nd->fd", product, out_cotangent, preferred_element_type=F32)
    grad_wout = grad_wout.astype(BF16)
    layer_out = (resid + jnp.dot(product, w_out, preferred_element_type=F32)).astype(BF16)
    grad_product = jnp.einsum("nd,fd->nf", out_cotangent, w_out, preferred_element_type=F32)
    grad_upper = gelu_pullback(grad_product * gating)[0]
    grad_proj = jnp.concatenate([grad_upper, grad_product * activated], axis=1).astype(BF16)
    grad_win = jnp.einsum("nd,nf->df", act_two, grad_proj, preferred_element_type=F32)
    grad_win = grad_win.astype(BF16)
    grad_proj, grad_win, grad_wout = lax.optimization_barrier((grad_proj, grad_win, grad_wout))
    grad_act_two = jnp.einsum("nf,df->nd", grad_proj, w_in, preferred_element_type=F32)
    grad_norm_two, grad_gain_two = norm_backward(grad_act_two, gain_two, scaled_two, inverse_two)
    grad_resid = out_cotangent.astype(F32) + grad_norm_two
    grad_mixed = grad_resid.astype(BF16)
    grad_attended = jnp.einsum("ne,de->nd", grad_mixed, w_attn, preferred_element_type=F32)
    grad_attended = grad_attended.astype(BF16)
    grad_wattn = jnp.einsum("nd,ne->de", attended, grad_mixed, preferred_element_type=F32)
    grad_wattn = grad_wattn.astype(BF16)

    dq, dk, dv, dlk, dlv, dhk, dhv = attention_back(
        qkv, low, high, bias, grad_attended, lse, cosine, sine
    )
    from_above = passed_along(jnp.concatenate([dlk, dlv], axis=1), STREAM, -1)
    from_below = passed_along(jnp.concatenate([dhk, dhv], axis=1), STREAM, 1)
    grad_qkv = join_grads(dq, dk, dv, from_below, from_above, cosine, sine)
    grad_wqkv = jnp.einsum("nd,nf->df", act_one, grad_qkv, preferred_element_type=F32)
    grad_wqkv = grad_wqkv.astype(BF16)
    grad_act_one = jnp.einsum("nf,df->nd", grad_qkv, w_qkv, preferred_element_type=F32)
    grad_norm_one, grad_gain_one = norm_backward(grad_act_one, gain_one, scaled_one, inverse_one)
    grad_tokens = grad_resid + grad_norm_one
    gains = jnp.stack([grad_gain_one, grad_gain_two])
    gains = lax.psum(gains, "dp")
    gains = lax.psum_scatter(gains, "fsdp", scatter_dimension=1, tiled=True)
    return (
        layer_out,
        grad_tokens,
        gains[0],
        summed(grad_wqkv),
        summed(grad_wattn),
        gains[1],
        summed(grad_win),
        summed(grad_wout),
    )


def solution(mesh):
    placed = (
        P(("dp", "fsdp"), None),
        P(("dp", "fsdp")),
        P(("dp", "fsdp")),
        P("fsdp"),
        P("fsdp", None),
        P("fsdp", None),
        P("fsdp"),
        P("fsdp", None),
        P("fsdp", None),
        P(("dp", "fsdp"), None),
    )
    return jax.shard_map(
        body,
        mesh=mesh,
        in_specs=placed,
        out_specs=(
            P(("dp", "fsdp"), None),
            P(("dp", "fsdp"), None),
            P("fsdp"),
            P("fsdp", None),
            P("fsdp", None),
            P("fsdp"),
            P("fsdp", None),
            P("fsdp", None),
        ),
        check_vma=False,
    )
```

time: 1300 us -> 876 us (0.67)
  local copies, waits for them, and re-layouts: 242 us -> 21.9 us
  matrix products: 302 us -> 158 us
  other arithmetic: 160 us -> 62.7 us
  Pallas kernels: 0 us -> 72.2 us
  loops' own time: 14.3 us -> 0 us
  waiting for transfers between devices: 491 us -> 478 us
    dot_general x26 -> x11, matrix products: 302 us -> 158 us  [the longest x1 36.3 us: body(): jnp.einsum('nd,fd->nf', out_cotangent, w_out, preferred_element_type=F32)]
    dynamic_update_slice x10 -> x0, local copies, waits for them, and re-layouts: 135 us -> none  [the longest x8 84.9 us: body(): attended, log_totals = lax.map(block_forward, block_rows)]
    pallas_call x0 -> x4, Pallas kernels: none -> 72.2 us  [the longest x1 27.7 us: attention_back(): pl.pallas_call(attend_back_kernel, grid=(pairs,), in_specs=[column(0), co...]
    psum x1, waiting for transfers between devices: 154 us -> 202 us  [summed(): part = lax.psum(part, 'dp', axis_index_groups=same_core())]
    slice x13 -> x4, local copies, waits for them, and re-layouts: 43.6 us -> 3.03 us  [the longest x1 1.78 us: body(): high = passed_along(qkv[:HALF, model_width:], STREAM, -1)]
    convert_element_type x11 -> x8, other arithmetic: 56.9 us -> 21.5 us  [the longest x4 20.8 us: summed(): return whole.astype(F32)]
    all_gather x4 -> x8, waiting for transfers between devices: 134 us -> 104 us  [the longest x4 94.2 us: gathered(): lax.all_gather(mine, STREAM, axis=0, tiled=True, axis_index_groups=quads())]
    reduce_scatter x4, waiting for transfers between devices: 185 us -> 161 us  [summed(): lax.psum_scatter(grad, STREAM, scatter_dimension=0, tiled=True, axis_inde...]
  transfers between devices with their start and end apart: 13 -> 18, of which waited for: 9 -> 10; matrix products, arithmetic and copies ran while one was open for 47% -> 12% of each run, Pallas kernels for 0% -> 8%
where the time goes in v1:
time: 876 us; the launch traced here: 869 us
  waiting for transfers between devices  478 us (55%)
  matrix products  158 us (18%)
  Pallas kernels  72.2 us (8%)
  other arithmetic  62.7 us (7%)
  blocking collectives  50.2 us (6%)
  local copies, waits for them, and re-layouts  21.9 us (2%)
  between operations  14.7 us (2%)
  starting transfers between devices  12.3 us (1%)
    psum x1, waiting for transfers between devices, summed(): part = lax.psum(part, 'dp', axis_index_groups=same_core())  202 us
    reduce_scatter x4, waiting for transfers between devices, summed(): lax.psum_scatter(grad, STREAM, scatter_dimension=0, tiled=True, axis_inde...  161 us
    all_gather x4, waiting for transfers between devices, gathered(): lax.all_gather(mine, STREAM, axis=0, tiled=True, axis_index_groups=quads())  94.2 us
    dot_general x1, matrix products, body(): jnp.einsum('nd,fd->nf', out_cotangent, w_out, preferred_element_type=F32)  36.3 us
    psum x1, blocking collectives, body(): gains = lax.psum(gains, 'dp')  32.6 us
    pallas_call x1, Pallas kernels, attention_back(): pl.pallas_call(attend_back_kernel, grid=(pairs,), in_specs=[column(0), co...  27.7 us
    dot_general x1, matrix products, body(): projected = jnp.dot(act_two, w_in, preferred_element_type=F32)  20.8 us
    convert_element_type x4, other arithmetic, summed(): return whole.astype(F32)  20.8 us
  transfers between devices with their start and end apart: 18, of which 10 were waited for; matrix products, arithmetic and copies ran while one was open for 12% of the time, Pallas kernels for 8%

profile of v1, /device:TPU:0, one launch (start us, length us, event | category | flops | bytes accessed | tf_op | source)
XLA Modules:
  0.0 869.5 jit_solution(16271472708324818795)
XLA Ops:
  7.2 1.8 copy-done
  10.4 1.9 constant_dynamic-slice_fusion.2
  12.4 3.5 constant_dynamic-slice_fusion.1
  15.9 2.6 constant_dynamic-slice_fusion
  19.2 5.4 all-gather
  24.6 1.9 fusion.36
  30.5 29.1 %all-gather.11.cloned.1.call-done.w_ref = bf16[1024,3072]{1,0:T(8,128)(2,1)} async-done(((bf16[256,3072]{1,0:T(8,128)(2,1)}), bf16[1024,3072]{1,0:T(8,128)(2,1)}) %all-gather.11.cloned.1.call-update) | async-done | bytes 6291472 | tf_op jit(solution)/shard_map/all_gather | solution.py:341
  59.6 14.7 %shard_map.161.q_ref.k_ref.v_ref = bf16[1024,3072]{1,0:T(8,128)(2,1)} custom-call(bf16[1024,1024]{1,0:T(8,128)(2,1)S(1)} %fusion.14.act_ref, bf16[1024,3072]{1,0:T(8,128)(2,1)} %all-gather.11.cloned.1.call-done.w_ref, f32[1024,128]{1,0:T(8,128)S(1)} %get-tuple-element.66.cos_ref, f32[1024,128]{1,0:T(8,128)S(1)} %get-tuple-element.67.sin_ref), custom_call_target="tpu_custom_call" | custom-call | flops 6442450944 | bytes 14680064 | tf_op jit(solution)/shard_map/pallas_call | solution.py:91
  74.3 1.8 fusion.39
  76.0 1.3 collective-permute-start.1
  77.3 4.6 collective-permute-start
  81.9 12.3 %all-gather.1 = bf16[2,1,512]{2,1,0:T(2,128)(2,1)S(1)} all-gather(bf16[1,1,512]{2,1,0:T(2,128)(2,1)S(1)} %reshape.83), channel_id=1, replica_groups=mesh['dp'=16,'fsdp'=2] {'fsdp'}, dimensions={0}, use_global_device_ids=true | all-gather | bytes 3072 | tf_op jit(solution)/shard_map/all_gather | solution.py:367
  95.2 13.5 %shard_map.162 = (bf16[1024,1024]{1,0:T(8,128)(2,1)S(1)}, f32[8,8,256]{2,1,0:T(8,128)S(1)}) custom-call(bf16[1024,3072]{1,0:T(8,128)(2,1)} %shard_map.161.q_ref.k_ref.v_ref, bf16[1024,3072]{1,0:T(8,128)(2,1)} %shard_map.161.q_ref.k_ref.v_ref, bf16[1024,3072]{1,0:T(8,128)(2,1)} %shard_map.161.q_ref.k_ref.v_ref, ...), custom_call_target="tpu_custom_call" | custom-call | flops 4294967296 | bytes 8388608 | tf_op jit(solution)/shard_map/pallas_call | solution.py:149
  109.6 5.4 fusion.41
  115.1 2.0 copy-done.21
  117.6 42.7 %all-gather.15.cloned.1.call-done = bf16[1024,5248]{1,0:T(8,128)(2,1)} async-done(((bf16[256,5248]{1,0:T(8,128)(2,1)}), bf16[1024,5248]{1,0:T(8,128)(2,1)}) %all-gather.15.cloned.1.call-update) | async-done | bytes 10747920 | tf_op jit(solution)/shard_map/all_gather | solution.py:341
  160.4 20.8 %fusion.37 = f32[1024,5248]{1,0:T(8,128)} fusion(bf16[1024,5248]{1,0:T(8,128)(2,1)} %all-gather.15.cloned.1.call-done, f32[1024,1024]{1,0:T(8,128)} %copy-done.21, f32[1024]{0:T(1024)S(1)} %bitcast.52, f32[1024]{0:T(1024)S(1)} %add_rsqrt_fusion, f32[1024]{0:T(1024)S(1)} %broadcast_multiply_fusion.4), kind=kOutput, calls=%fused_computation.95 | convolution fusion | flops 11010048000 | bytes 36450304 | tf_op jit(solution)/shard_map/dot_general | solution.py:396
  181.2 22.4 %all-gather.17.cloned.1.call-done = bf16[2624,1024]{1,0:T(8,128)(2,1)} async-done(((bf16[656,1024]{1,0:T(8,128)(2,1)}), bf16[2624,1024]{1,0:T(8,128)(2,1)}) %all-gather.17.cloned.1.call-update) | async-done | bytes 5373968 | tf_op jit(solution)/shard_map/all_gather | solution.py:341
  203.6 36.3 %add_convert_fusion = (bf16[1024,2624]{1,0:T(8,128)(2,1)}, f32[1024,2624]{1,0:T(8,128)S(1)}, f32[2624,1024]{0,1:T(8,128)}) fusion(f32[1024,5248]{1,0:T(8,128)} %fusion.37, bf16[2624,1024]{1,0:T(8,128)(2,1)} %all-gather.17.cloned.1.call-done, bf16[1024,1024]{1,0:T(8,128)(2,1)S(1)} %copy-done.25), kind=kOutput, calls=%fused_computation.6 | convolution fusion | flops 5699076096 | bytes 55836672 | tf_op jit(solution)/shard_map/nd,fd->nf/dot_general | solution.py:403
  239.8 16.6 %fusion.1 = (bf16[1024,2624]{1,0:T(8,128)(2,1)}, bf16[1024,2624]{1,0:T(8,128)(2,1)}) fusion(f32[2624,1024]{0,1:T(8,128)} %get-tuple-element.63, f32[1024,2624]{1,0:T(8,128)S(1)} %get-tuple-element.43, f32[1024,5248]{1,0:T(8,128)} %fusion.37), kind=kLoop, calls=%fused_computation.5 | loop fusion | flops 16121856 | bytes 53739520 | tf_op jit(solution)/shard_map/convert.1
  256.5 10.1 %convolution_convert_fusion.2 = bf16[2624,1024]{1,0:T(8,128)(2,1)} fusion(bf16[1024,2624]{1,0:T(8,128)(2,1)} %get-tuple-element.45, bf16[1024,1024]{1,0:T(8,128)(2,1)S(1)} %copy-done.25), kind=kOutput, calls=%fused_computation.28 | convolution fusion | flops 5505613824 | bytes 12845056 | tf_op jit(solution)/shard_map/nf,nd->fd/dot_general | solution.py:400
  266.6 12.0 %pad_maximum_fusion = bf16[1024,5248]{1,0:T(8,128)(2,1)} fusion(bf16[1024,2624]{1,0:T(8,128)(2,1)} %get-tuple-element.44, bf16[1024,2624]{1,0:T(8,128)(2,1)} %get-tuple-element.42), kind=kLoop, calls=%fused_computation.21 | loop fusion | flops 21495808 | bytes 21495808 | tf_op jit(solution)/shard_map/concatenate | solution.py:405
  278.6 18.7 %convolution_convert_fusion = bf16[1024,5248]{1,0:T(8,128)(2,1)} fusion(bf16[1024,5248]{1,0:T(8,128)(2,1)} %pad_maximum_fusion, f32[1024,1024]{1,0:T(8,128)S(1)} %copy-done.22, f32[1024]{0:T(1024)S(1)} %bitcast.53, f32[1024]{0:T(1024)S(1)} %add_rsqrt_fusion, f32[1024]{0:T(1024)S(1)} %broadcast_multiply_fusion.4), kind=kOutput, calls=%fused_computation.1 | convolution fusion | flops 11015421952 | bytes 25702400 | tf_op jit(solution)/shard_map/nd,nf->df/dot_general | solution.py:406
  297.2 20.2 %multiply_reduce_fusion = (f32[1024]{0:T(1024)S(1)}, f32[1024]{0:T(1024)S(1)}, f32[1024]{0:T(1024)S(1)}, f32[1024,1024]{1,0:T(8,128)}) fusion(f32[1024,1024]{1,0:T(8,128)} %copy-done.21, f32[1024]{0:T(1024)S(1)} %add_rsqrt_fusion, f32[1024]{0:T(1024)S(1)} %broadcast_multiply_fusion.4, f32[1024]{0:T(1024)S(1)} %bitcast.54, ...), kind=kOutput, calls=%fused_computation.42 | convolution fusion | flops 11014239232 | bytes 29908992 | tf_op jit(solution)/shard_map/nf,df->nd/dot_general | solution.py:409
  317.5 3.4 multiply_add_fusion
  320.9 2.1 copy-done.19
  323.0 3.9 convolution_convert_fusion.3
  327.6 6.7 convolution_convert_fusion.4.do_ref
  334.3 27.7 %shard_map.163 = (bf16[1024,1024]{1,0:T(8,128)(2,1)S(1)}, f32[1024,1024]{1,0:T(8,128)}, f32[1024,1024]{1,0:T(8,128)}, bf16[64,1024]{1,0:T(8,128)(2,1)S(1)}, bf16...) custom-call(bf16[1024,3072]{1,0:T(8,128)(2,1)} %shard_map.161.q_ref.k_ref.v_ref, ...), custom_call_target="tpu_custom_call" | custom-call | flops 10737418240 | bytes 20971520 | tf_op jit(solution)/shard_map/pallas_call | solution.py:226
  362.0 1.3 collective-permute-start.3
  363.4 4.6 collective-permute-start.2
  367.9 5.1 collective-permute-done.3.hi_ref
  373.1 2.8 collective-permute-done.2.lo_ref
  375.9 16.4 %shard_map.164 = bf16[1024,3072]{1,0:T(8,128)(2,1)} custom-call(bf16[1024,1024]{1,0:T(8,128)(2,1)S(1)} %get-tuple-element.23.dq_ref, f32[1024,1024]{1,0:T(8,128)} %get-tuple-element.24.dk_ref, f32[1024,1024]{1,0:T(8,128)} %get-tuple-element.25.dv_ref, bf16[64,2048]{1,0:T(8,128)(2,1)S(1)} %collective-permute-done.2.lo_ref, ...), custom_call_target="tpu_custom_call" | custom-call | flops 8388608 | bytes 16777216 | tf_op jit(solution)/shard_map/pallas_call | solution.py:286
  392.3 11.4 %convolution_convert_fusion.1 = bf16[1024,3072]{1,0:T(8,128)(2,1)} fusion(bf16[1024,1024]{1,0:T(8,128)(2,1)S(1)} %copy-done.9, bf16[1024,3072]{1,0:T(8,128)(2,1)} %shard_map.164), kind=kOutput, calls=%fused_computation.27 | convolution fusion | flops 6445596672 | bytes 14680064 | tf_op jit(solution)/shard_map/nd,nf->df/dot_general | solution.py:424
  404.6 9.3 %reduce-scatter.14.cloned.1.call-done = bf16[656,1024]{1,0:T(8,128)(2,1)} async-done(((bf16[2624,1024]{1,0:T(8,128)(2,1)}), bf16[656,1024]{1,0:T(8,128)(2,1)}) %reduce-scatter.14.cloned.1.call-update) | async-done | bytes 1343504 | tf_op jit(solution)/shard_map/reduce_scatter | solution.py:345
  413.9 61.5 %reduce-scatter.8.cloned.1.call-done = bf16[256,3072]{1,0:T(8,128)(2,1)} async-done(((bf16[1024,3072]{1,0:T(8,128)(2,1)}), bf16[256,3072]{1,0:T(8,128)(2,1)}) %reduce-scatter.8.cloned.1.call-update) | async-done | bytes 1572880 | tf_op jit(solution)/shard_map/reduce_scatter | solution.py:345
  475.4 89.8 %reduce-scatter.12.cloned.1.call-done = bf16[256,5248]{1,0:T(8,128)(2,1)} async-done(((bf16[1024,5248]{1,0:T(8,128)(2,1)}), bf16[256,5248]{1,0:T(8,128)(2,1)}) %reduce-scatter.12.cloned.1.call-update) | async-done | bytes 2686992 | tf_op jit(solution)/shard_map/reduce_scatter | solution.py:345
  565.3 12.6 %fusion.19 = (f32[1024]{0:T(1024)S(1)}, f32[1024]{0:T(1024)S(1)}, f32[1024]{0:T(1024)S(1)}, f32[1024,1024]{1,0:T(8,128)}) fusion(bf16[1024,1024]{1,0:T(8,128)(2,1)S(1)} %copy-done.18, f32[1024]{0:T(1024)S(1)} %copy-done.33, f32[1024]{0:T(1024)S(1)} %copy-done.29, f32[1024]{0:T(1024)S(1)} %bitcast.49, bf16[1024,3072]{1,0:T(8,128)(2,1)} %shard_map.164, ...), kind=kOutput, calls=%fused_computation.40 | convolution fusion | flops 6451885056 | bytes 18898944 | tf_op jit(solution)/shard_map/nf,df->nd/dot_general | solution.py:426
  579.1 202.3 %all-reduce.5.cloned.1.call-done = (bf16[256,3072]{1,0:T(8,128)(2,1)}, bf16[256,1024]{1,0:T(8,128)(2,1)}, bf16[256,5248]{1,0:T(8,128)(2,1)}, bf16[656,1024]{1,0:T(8,128)(2,1)}) async-done(((bf16[256,3072]{1,0:T(8,128)(2,1)}, bf16[256,1024]{1,0:T(8,128)(2,1)}, bf16[256,5248]{1,0:T(8,128)(2,1)}, bf16[656,1024]{1,0:T(8,128)(2,1)}), (bf16[256,3072]{1,0:T(8,128)(2,1)}, bf16[256,1024]{1,0:T(8,128)(2,1)}, ...) | async-done | bytes 6127632 | tf_op jit(solution)/shard_map/psum | solution.py:348
  783.3 11.6 %add_convert_fusion.1 = bf16[1024,1024]{1,0:T(8,128)(2,1)} fusion(f32[1024,1024]{1,0:T(8,128)} %copy-done.21, bf16[1024,2624]{1,0:T(8,128)(2,1)} %get-tuple-element.45, bf16[2624,1024]{1,0:T(8,128)(2,1)} %all-gather.17.cloned.1.call-done), kind=kOutput, calls=%fused_computation.45 | convolution fusion | flops 5505024000 | bytes 17039360 | tf_op jit(solution)/shard_map/dot_general | solution.py:402
  794.9 3.1 fusion.18
  799.1 32.6 %psum.40 = f32[2,512]{1,0:T(2,128)S(1)} all-reduce(f32[2,512]{1,0:T(2,128)S(1)} %copy.42), channel_id=1, replica_groups=mesh['dp'=16,'fsdp'=2] {'dp'}, use_global_device_ids=true, to_apply=%region_10.11 | all-reduce | flops 1024 | bytes 8192 | tf_op jit(solution)/shard_map/psum | solution.py:430
  832.3 3.0 convert_element_type.74
  835.2 4.8 convert_element_type.76
  840.1 5.5 convert_element_type.72
  845.6 9.7 %all-gather.23.cloned.1.call-done = bf16[512,5248]{1,0:T(8,128)(2,1)} async-done(((bf16[256,5248]{1,0:T(8,128)(2,1)}), bf16[512,5248]{1,0:T(8,128)(2,1)}) %all-gather.23.cloned.1.call-update) | async-done | bytes 5373968 | tf_op jit(solution)/shard_map/all_gather | solution.py:349
  855.3 7.4 convert_element_type.75
  (139 shorter events, 14.8 us)
Async XLA Ops:
  7.2 52.4 %all-gather.11.cloned.1.call-start = ((), (), s32[]{:S(2)}) async-start(), calls=%async_computation.5 | async-start | bytes 7864320 | tf_op jit(solution)/shard_map/all_gather | solution.py:341
  10.3 99.3 %all-gather.13.cloned.1.call-start = ((), (), s32[]{:S(2)}) async-start(), calls=%async_computation.6 | async-start | bytes 2621440 | tf_op jit(solution)/shard_map/all_gather | solution.py:341
  12.3 6.4 copy-start.27
  12.3 6.9 copy-start.35
  12.3 12.3 %copy-start.34 = (s32[1024]{0:T(1024)S(1)}, s32[1024]{0:T(1024)}, u32[]{:S(2)}) copy-start(s32[1024]{0:T(1024)} %param.12) | copy-start | bytes 12292
  12.3 148.0 %all-gather.15.cloned.1.call-start = ((), (), s32[]{:S(2)}) async-start(), calls=%async_computation.7 | async-start | bytes 13434880 | tf_op jit(solution)/shard_map/all_gather | solution.py:341
  15.8 11.6 %copy-start.16 = (bf16[1024,1024]{1,0:T(8,128)(2,1)S(1)}, bf16[1024,1024]{1,0:T(8,128)(2,1)}, u32[]{:S(2)}) copy-start(bf16[1024,1024]{1,0:T(8,128)(2,1)} %param.10) | copy-start | bytes 6291460
  15.9 187.7 %all-gather.17.cloned.1.call-start = ((), (), s32[]{:S(2)}) async-start(), calls=%async_computation.8 | async-start | bytes 6717440 | tf_op jit(solution)/shard_map/all_gather | solution.py:341
  18.6 386.0 %reduce-scatter.10.cloned.1.call-start = ((), (), s32[]{:S(2)}) async-start(), calls=%async_computation.11 | async-start | bytes 2621440 | tf_op jit(solution)/shard_map/reduce_scatter | solution.py:345
  18.6 11.2 %copy-start.17 = (bf16[1024,1024]{1,0:T(8,128)(2,1)S(1)}, bf16[1024,1024]{1,0:T(8,128)(2,1)}, u32[]{:S(2)}) copy-start(bf16[1024,1024]{1,0:T(8,128)(2,1)} %param.10) | copy-start | bytes 6291460
  27.4 46.8 %copy-start.4 = (f32[1024,128]{1,0:T(8,128)}, f32[1024,128]{1,0:T(8,128)S(1)}, u32[]{:S(2)}) copy-start(f32[1024,128]{1,0:T(8,128)S(1)} %get-tuple-element.66.cos_ref) | copy-start | bytes 1572868
  27.4 46.8 %copy-start.6 = (f32[1024,128]{1,0:T(8,128)}, f32[1024,128]{1,0:T(8,128)S(1)}, u32[]{:S(2)}) copy-start(f32[1024,128]{1,0:T(8,128)S(1)} %get-tuple-element.67.sin_ref) | copy-start | bytes 1572868
  30.5 43.8 %copy-start.8 = (bf16[1024,1024]{1,0:T(8,128)(2,1)}, bf16[1024,1024]{1,0:T(8,128)(2,1)S(1)}, u32[]{:S(2)}) copy-start(bf16[1024,1024]{1,0:T(8,128)(2,1)S(1)} %fusion.14.act_ref) | copy-start | bytes 6291460
  59.6 22.3 %copy-start.36 = (bf16[512]{0:T(512)(128)(2,1)S(1)}, bf16[512]{0:T(512)(128)(2,1)}, u32[]{:S(2)}) copy-start(bf16[512]{0:T(512)(128)(2,1)} %param.16) | copy-start | bytes 3076
  76.0 19.1 %collective-permute-start.1 = (bf16[64,2048]{1,0:T(8,128)(2,1)}, bf16[64,2048]{1,0:T(8,128)(2,1)S(1)}, u32[]{:S(2)}, u32[]{:S(2)}) collective-permute-start(bf16[64,2048]{1,0:T(8,128)(2,1)} %get-tuple-element.46), channel_id=1, source_target_pairs={{1,0},{2,1},{3,2},{4,3},{5,4},{6,5},{7,6},{8,7},{9,8},{10,9},{11,1... | collective-permute-start | bytes 786440 | tf_op jit(solution)/shard_map/ppermute | solution.py:26
  77.3 17.9 %collective-permute-start = (bf16[64,2048]{1,0:T(8,128)(2,1)S(1)}, bf16[64,2048]{1,0:T(8,128)(2,1)S(1)}, u32[]{:S(2)}, u32[]{:S(2)}) collective-permute-start(bf16[64,2048]{1,0:T(8,128)(2,1)S(1)} %get-tuple-element.47), channel_id=1, source_target_pairs={{0,1},{1,2},{2,3},{3,4},{4,5},{5,6},{6,7},{7,8},{8,9},{9,10},{10,1... | collective-permute-start | bytes 786440 | tf_op jit(solution)/shard_map/ppermute | solution.py:26
  95.2 13.5 %copy-start.10 = (bf16[64,2048]{1,0:T(8,128)(2,1)}, bf16[64,2048]{1,0:T(8,128)(2,1)S(1)}, u32[]{:S(2)}) copy-start(bf16[64,2048]{1,0:T(8,128)(2,1)S(1)} %collective-permute-done.1.hk_ref.hv_ref) | copy-start | bytes 786436
  95.2 13.5 %copy-start.12 = (bf16[64,2048]{1,0:T(8,128)(2,1)}, bf16[64,2048]{1,0:T(8,128)(2,1)S(1)}, u32[]{:S(2)}) copy-start(bf16[64,2048]{1,0:T(8,128)(2,1)S(1)} %collective-permute-done.lk_ref.lv_ref) | copy-start | bytes 786436
  109.6 5.4 copy-start.14
  160.4 43.2 %copy-start.25 = (bf16[1024,1024]{1,0:T(8,128)(2,1)S(1)}, bf16[1024,1024]{1,0:T(8,128)(2,1)}, u32[]{:S(2)}) copy-start(bf16[1024,1024]{1,0:T(8,128)(2,1)} %param.19) | copy-start | bytes 6291460
  266.6 12.0 %copy-start.22 = (f32[1024,1024]{1,0:T(8,128)S(1)}, f32[1024,1024]{1,0:T(8,128)}, u32[]{:S(2)}) copy-start(f32[1024,1024]{1,0:T(8,128)} %copy-done.21) | copy-start | bytes 12582916
  297.2 20.2 %copy-start.23 = (f32[1024,1024]{1,0:T(8,128)S(1)}, f32[1024,1024]{1,0:T(8,128)}, u32[]{:S(2)}) copy-start(f32[1024,1024]{1,0:T(8,128)} %copy-done.21) | copy-start | bytes 12582916
  297.2 20.2 %copy-start.26 = (bf16[1024,1024]{1,0:T(8,128)(2,1)S(1)}, bf16[1024,1024]{1,0:T(8,128)(2,1)}, u32[]{:S(2)}) copy-start(bf16[1024,1024]{1,0:T(8,128)(2,1)} %param.19) | copy-start | bytes 6291460
  317.4 5.6 copy-start.15
  326.9 87.0 %reduce-scatter.14.cloned.1.call-start = ((), (), s32[]{:S(2)}) async-start(), calls=%async_computation.15 | async-start | bytes 6717440 | tf_op jit(solution)/shard_map/reduce_scatter | solution.py:345
  327.5 6.8 copy-start.3
  327.5 6.8 copy-start.5
  327.5 6.8 copy-start.7
  327.5 6.8 copy-start.11
  327.5 6.8 copy-start.13
  327.5 147.9 %reduce-scatter.8.cloned.1.call-start = ((), (), s32[]{:S(2)}) async-start(), calls=%async_computation.9 | async-start | bytes 7864320 | tf_op jit(solution)/shard_map/reduce_scatter | solution.py:345
  362.0 11.0 %collective-permute-start.3 = (bf16[64,2048]{1,0:T(8,128)(2,1)S(1)}, bf16[64,2048]{1,0:T(8,128)(2,1)S(1)}, u32[]{:S(2)}, u32[]{:S(2)}) collective-permute-start(bf16[64,2048]{1,0:T(8,128)(2,1)S(1)} %pad_maximum_fusion.4), channel_id=1, source_target_pairs={{1,0},{2,1},{3,2},{4,3},{5,4},{6,5},{7,6},{8,7},{9,8},{10,9},{11,1... | collective-permute-start | bytes 786440 | tf_op jit(solution)/shard_map/ppermute | solution.py:26
  363.4 12.5 %collective-permute-start.2 = (bf16[64,2048]{1,0:T(8,128)(2,1)S(1)}, bf16[64,2048]{1,0:T(8,128)(2,1)S(1)}, u32[]{:S(2)}, u32[]{:S(2)}) collective-permute-start(bf16[64,2048]{1,0:T(8,128)(2,1)S(1)} %pad_maximum_fusion.3), channel_id=1, source_target_pairs={{0,1},{1,2},{2,3},{3,4},{4,5},{5,6},{6,7},{7,8},{8,9},{9,10},{10,1... | collective-permute-start | bytes 786440 | tf_op jit(solution)/shard_map/ppermute | solution.py:26
  375.9 16.4 %copy-start.9 = (bf16[1024,1024]{1,0:T(8,128)(2,1)S(1)}, bf16[1024,1024]{1,0:T(8,128)(2,1)}, u32[]{:S(2)}) copy-start(bf16[1024,1024]{1,0:T(8,128)(2,1)} %copy-done.8) | copy-start | bytes 6291460
  403.7 161.5 %reduce-scatter.12.cloned.1.call-start = ((), (), s32[]{:S(2)}) async-start(), calls=%async_computation.13 | async-start | bytes 13434880 | tf_op jit(solution)/shard_map/reduce_scatter | solution.py:345
  404.5 160.8 %copy-start.18 = (bf16[1024,1024]{1,0:T(8,128)(2,1)S(1)}, bf16[1024,1024]{1,0:T(8,128)(2,1)}, u32[]{:S(2)}) copy-start(bf16[1024,1024]{1,0:T(8,128)(2,1)} %param.10) | copy-start | bytes 6291460
  404.5 160.8 %copy-start.29 = (f32[1024]{0:T(1024)S(1)}, f32[1024]{0:T(1024)}, u32[]{:S(2)}) copy-start(f32[1024]{0:T(1024)} %copy-done.28) | copy-start | bytes 12292
  404.5 160.8 %copy-start.31 = (f32[2,1,512]{2,1,0:T(1,128)S(1)}, f32[2,1,512]{2,1,0:T(1,128)}, u32[]{:S(2)}) copy-start(f32[2,1,512]{2,1,0:T(1,128)} %copy-done.30) | copy-start | bytes 12292
  404.5 160.8 %copy-start.33 = (f32[1024]{0:T(1024)S(1)}, f32[1024]{0:T(1024)}, u32[]{:S(2)}) copy-start(f32[1024]{0:T(1024)} %copy-done.32) | copy-start | bytes 12292
  404.5 376.9 %all-reduce.5.cloned.1.call-start = ((), (), s32[]{:S(2)}) async-start(), calls=%async_computation.18 | async-start | bytes 12255232 | tf_op jit(solution)/shard_map/psum | solution.py:348
  565.3 232.8 %reduce-scatter.16.cloned.1.call-start = ((), (), s32[]{:S(2)}) async-start(), calls=%async_computation.17 | async-start | bytes 786432
  579.0 253.2 %all-gather.21.cloned.1.call-start = ((), (), s32[]{:S(2)}) async-start(), calls=%async_computation.12 | async-start | bytes 1572864 | tf_op jit(solution)/shard_map/all_gather | solution.py:349
  781.4 53.9 %all-gather.25.cloned.1.call-start = ((), (), s32[]{:S(2)}) async-start(), calls=%async_computation.16 | async-start | bytes 4030464 | tf_op jit(solution)/shard_map/all_gather | solution.py:349
  782.0 58.1 %all-gather.19.cloned.1.call-start = ((), (), s32[]{:S(2)}) async-start(), calls=%async_computation.10 | async-start | bytes 4718592 | tf_op jit(solution)/shard_map/all_gather | solution.py:349
  782.7 72.6 %all-gather.23.cloned.1.call-start = ((), (), s32[]{:S(2)}) async-start(), calls=%async_computation.14 | async-start | bytes 8060928 | tf_op jit(solution)/shard_map/all_gather | solution.py:349
  783.3 11.6 %copy-start.20 = (f32[1024,1024]{1,0:T(8,128)S(1)}, f32[1024,1024]{1,0:T(8,128)}, u32[]{:S(2)}) copy-start(f32[1024,1024]{1,0:T(8,128)} %copy-done.19) | copy-start | bytes 12582916
  783.3 11.6 %copy-start.24 = (f32[1024,1024]{1,0:T(8,128)S(1)}, f32[1024,1024]{1,0:T(8,128)}, u32[]{:S(2)}) copy-start(f32[1024,1024]{1,0:T(8,128)} %get-tuple-element.65) | copy-start | bytes 12582916
  840.1 22.7 %copy-start.1 = (bf16[512,3072]{1,0:T(8,128)(2,1)S(1)}, bf16[512,3072]{1,0:T(8,128)(2,1)}, u32[]{:S(2)}) copy-start(bf16[512,3072]{1,0:T(8,128)(2,1)} %param.14) | copy-start | bytes 9437188
  (7 other events, 13.0 us)
Sparse Core Ops, SparseCore 0:
  10.5 49.0 all-gather.10
  61.7 24.4 all-gather.12
  88.4 71.9 all-gather.14
  162.3 41.1 all-gather.16
  327.0 31.4 reduce-scatter.9
  361.6 52.2 reduce-scatter.13
  417.0 58.3 reduce-scatter.7
  478.2 86.9 reduce-scatter.11
  570.7 210.6 all-reduce.4
  784.0 13.4 reduce-scatter.15
  799.1 9.0 all-gather.20
  809.7 12.6 all-gather.24
  823.9 13.2 all-gather.18
  838.7 16.5 all-gather.22

commit v2 on v1

--- a/solution.py
+++ b/solution.py
@@ -327,27 +327,66 @@
     ]
 
 
-def chips():
-    return [[2 * m, 2 * m + 1] for m in range(lax.axis_size("dp") // 2)]
-
-
-def same_core():
-    return [[2 * m + c for m in range(lax.axis_size("dp") // 2)] for c in range(2)]
-
-
 def gathered(shard):
     half = shard.shape[0] // 2
     mine = lax.dynamic_slice_in_dim(shard, (lax.axis_index("dp") % 2) * half, half, 0)
     return lax.all_gather(mine, STREAM, axis=0, tiled=True, axis_index_groups=quads())
 
 
-def summed(grad):
-    part = lax.psum_scatter(
-        grad, STREAM, scatter_dimension=0, tiled=True, axis_index_groups=quads()
-    )
-    part = lax.psum(part, "dp", axis_index_groups=same_core())
-    whole = lax.all_gather(part, "dp", axis=0, tiled=True, axis_index_groups=chips())
-    return whole.astype(F32)
+def partners(axis, bit):
+    return [(i, i ^ (1 << bit)) for i in range(lax.axis_size(axis))]
+
+
+def halves(x, dim, axis, bit):
+    side = (lax.axis_index(axis) >> bit) % 2
+    size = x.shape[dim] // 2
+    keep = lax.dynamic_slice_in_dim(x, side * size, size, dim)
+    send = lax.dynamic_slice_in_dim(x, (1 - side) * size, size, dim)
+    return keep, send
+
+
+def halved(x, dim, axis, bit):
+    keep, send = halves(x, dim, axis, bit)
+    got = lax.ppermute(send, axis, partners(axis, bit))
+    return (keep.astype(F32) + got.astype(F32)).astype(BF16)
+
+
+def doubled(x, dim, axis, bit):
+    got = lax.ppermute(x, axis, partners(axis, bit))
+    side = (lax.axis_index(axis) >> bit) % 2
+    low = jnp.where(side == 0, x, got)
+    high = jnp.where(side == 0, got, x)
+    return jnp.concatenate([low, high], axis=dim)
+
+
+def over_cores(grad):
+    wide = lax.axis_size("fsdp")
+    rows, columns = grad.shape
+    return halved(grad.reshape(wide, rows // wide, columns), 1, "dp", 0)
+
+
+def over_fsdp(part):
+    if lax.axis_size("fsdp") == 2:
+        return halved(part, 0, "fsdp", 0)[0]
+    return lax.psum_scatter(part, "fsdp", scatter_dimension=0, tiled=True)[0]
+
+
+def over_rest(part, dim):
+    levels = lax.axis_size("dp").bit_length() - 1
+    for bit in range(1, levels):
+        part = halved(part, dim, "dp", bit)
+    for bit in reversed(range(1, levels)):
+        part = doubled(part, dim, "dp", bit)
+    return doubled(part, 0, "dp", 0).astype(F32)
+
+
+def summed_gains(gains):
+    for bit in range(lax.axis_size("dp").bit_length() - 1):
+        gains = gains + lax.ppermute(gains, "dp", partners("dp", bit))
+    if lax.axis_size("fsdp") == 2:
+        keep, send = halves(gains, 1, "fsdp", 0)
+        return keep + lax.ppermute(send, "fsdp", partners("fsdp", 0))
+    return lax.psum_scatter(gains, "fsdp", scatter_dimension=1, tiled=True)
 
 
 def body(
@@ -363,8 +402,8 @@
     out_cotangent,
 ):
     w_qkv = gathered(qkv_weight)
-    gain_one = lax.all_gather(attn_gain, "fsdp", axis=0, tiled=True)
-    gain_two = lax.all_gather(mlp_gain, "fsdp", axis=0, tiled=True)
+    gains = jnp.stack([attn_gain, mlp_gain])
+    gain_one, gain_two = lax.all_gather(gains, "fsdp", axis=1, tiled=True)
     w_attn = gathered(attn_out_weight)
     w_in = gathered(mlp_in_weight)
     w_out = gathered(mlp_out_weight)
@@ -415,6 +454,15 @@
     grad_wattn = jnp.einsum("nd,ne->de", attended, grad_mixed, preferred_element_type=F32)
     grad_wattn = grad_wattn.astype(BF16)
 
+    part_win = over_cores(grad_win)
+    part_wout = over_cores(grad_wout)
+    grad_attended, part_win, part_wout = lax.optimization_barrier(
+        (grad_attended, part_win, part_wout)
+    )
+    part_win = over_fsdp(part_win)
+    part_wout = over_fsdp(part_wout)
+    part_wattn = over_cores(grad_wattn)
+
     dq, dk, dv, dlk, dlv, dhk, dhv = attention_back(
         qkv, low, high, bias, grad_attended, lse, cosine, sine
     )
@@ -423,21 +471,23 @@
     grad_qkv = join_grads(dq, dk, dv, from_below, from_above, cosine, sine)
     grad_wqkv = jnp.einsum("nd,nf->df", act_one, grad_qkv, preferred_element_type=F32)
     grad_wqkv = grad_wqkv.astype(BF16)
+    grad_wqkv, part_win, part_wout, part_wattn, grad_qkv = lax.optimization_barrier(
+        (grad_wqkv, part_win, part_wout, part_wattn, grad_qkv)
+    )
+    part_wqkv = over_cores(grad_wqkv)
     grad_act_one = jnp.einsum("nf,df->nd", grad_qkv, w_qkv, preferred_element_type=F32)
     grad_norm_one, grad_gain_one = norm_backward(grad_act_one, gain_one, scaled_one, inverse_one)
     grad_tokens = grad_resid + grad_norm_one
-    gains = jnp.stack([grad_gain_one, grad_gain_two])
-    gains = lax.psum(gains, "dp")
-    gains = lax.psum_scatter(gains, "fsdp", scatter_dimension=1, tiled=True)
+    gains = summed_gains(jnp.stack([grad_gain_one, grad_gain_two]))
     return (
         layer_out,
         grad_tokens,
         gains[0],
-        summed(grad_wqkv),
-        summed(grad_wattn),
+        over_rest(over_fsdp(part_wqkv), 0),
+        over_rest(over_fsdp(part_wattn), 0),
         gains[1],
-        summed(grad_win),
-        summed(grad_wout),
+        over_rest(part_win, 0),
+        over_rest(part_wout, 1),
     )
 
 

time: 876 us -> 716 us (0.82)
  waiting for transfers between devices: 478 us -> 308 us
  blocking collectives: 50.2 us -> 5.24 us
  starting transfers between devices: 12.3 us -> 54.9 us
  other arithmetic: 62.7 us -> 79.1 us
  matrix products: 158 us -> 147 us
    psum x1 -> x0, waiting for transfers between devices: 202 us -> none  [summed(): part = lax.psum(part, 'dp', axis_index_groups=same_core())]
    ppermute x0 -> x41, waiting for transfers between devices: none -> 169 us  [the longest x20 83 us: halved(): got = lax.ppermute(send, axis, partners(axis, bit))]
    reduce_scatter x4 -> x0, waiting for transfers between devices: 161 us -> none  [summed(): lax.psum_scatter(grad, STREAM, scatter_dimension=0, tiled=True, axis_inde...]
    ppermute x0 -> x41, starting transfers between devices: none -> 45.2 us  [the longest x20 22.8 us: halved(): got = lax.ppermute(send, axis, partners(axis, bit))]
    ppermute x4, waiting for transfers between devices: 7.93 us -> 42.7 us  [passed_along(): return lax.ppermute(x, axis, pairs)]
    psum x1 -> x0, blocking collectives: 32.6 us -> none  [body(): gains = lax.psum(gains, 'dp')]
    all_gather x2 -> x1, blocking collectives: 17.6 us -> 5.24 us  [body(): gain_one, gain_two = lax.all_gather(gains, 'fsdp', axis=1, tiled=True)]
    all_gather x4 -> x0, waiting for transfers between devices: 9.71 us -> none  [summed(): lax.all_gather(part, 'dp', axis=0, tiled=True, axis_index_groups=chips())]
  transfers between devices with their start and end apart: 18 -> 49, of which waited for: 10 -> 30; matrix products, arithmetic and copies ran while one was open for 12% -> 20% of each run, Pallas kernels for 8% -> 10%
where the time goes in v2:
time: 716 us; the launch traced here: 710 us
  waiting for transfers between devices  308 us (43%)
  matrix products  147 us (21%)
  other arithmetic  79.1 us (11%)
  Pallas kernels  71.4 us (10%)
  starting transfers between devices  54.9 us (8%)
  local copies, waits for them, and re-layouts  28.6 us (4%)
  between operations  15.3 us (2%)
    all_gather x4, waiting for transfers between devices, gathered(): lax.all_gather(mine, STREAM, axis=0, tiled=True, axis_index_groups=quads())  96.5 us
    ppermute x20, waiting for transfers between devices, halved(): got = lax.ppermute(send, axis, partners(axis, bit))  83 us
    ppermute x16, waiting for transfers between devices, doubled(): got = lax.ppermute(x, axis, partners(axis, bit))  52.3 us
    ppermute x4, waiting for transfers between devices, passed_along(): return lax.ppermute(x, axis, pairs)  42.7 us
    dot_general x1, matrix products, body(): jnp.einsum('nd,fd->nf', out_cotangent, w_out, preferred_element_type=F32)  37.5 us
    ppermute x4, waiting for transfers between devices, summed_gains(): gains = gains + lax.ppermute(gains, 'dp', partners('dp', bit))  33.8 us
    pallas_call x1, Pallas kernels, attention_back(): pl.pallas_call(attend_back_kernel, grid=(pairs,), in_specs=[column(0), co...  27.1 us
    ppermute x20, starting transfers between devices, halved(): got = lax.ppermute(send, axis, partners(axis, bit))  22.8 us
  transfers between devices with their start and end apart: 49, of which 30 were waited for; matrix products, arithmetic and copies ran while one was open for 20% of the time, Pallas kernels for 10%

profile of v2, /device:TPU:0, one launch (start us, length us, event | category | flops | bytes accessed | tf_op | source)
XLA Modules:
  0.0 709.7 jit_solution(16716277246195568730)
XLA Ops:
  12.3 3.5 constant_dynamic-slice_fusion.21
  22.0 5.2 all_gather.15
  30.4 29.2 %all-gather.5.cloned.1.call-done.w_ref = bf16[1024,3072]{1,0:T(8,128)(2,1)} async-done(((bf16[256,3072]{1,0:T(8,128)(2,1)}), bf16[1024,3072]{1,0:T(8,128)(2,1)}) %all-gather.5.cloned.1.call-update) | async-done | bytes 6291472 | tf_op jit(solution)/shard_map/all_gather | solution.py:333
  59.6 14.6 %shard_map.161.q_ref.k_ref.v_ref = bf16[1024,3072]{1,0:T(8,128)(2,1)} custom-call(bf16[1024,1024]{1,0:T(8,128)(2,1)S(1)} %fusion.14.act_ref, bf16[1024,3072]{1,0:T(8,128)(2,1)} %all-gather.5.cloned.1.call-done.w_ref, f32[1024,128]{1,0:T(8,128)S(1)} %get-tuple-element.112.cos_ref, f32[1024,128]{1,0:T(8,128)S(1)} %get-tuple-element.113.sin_ref), custom_call_target="tpu_custom_call" | custom-call | flops 6442450944 | bytes 14680064 | tf_op jit(solution)/shard_map/pallas_call | solution.py:91
  81.0 8.3 %collective-permute-done.lk_ref.lv_ref = bf16[64,2048]{1,0:T(8,128)(2,1)S(1)} collective-permute-done((bf16[64,2048]{1,0:T(8,128)(2,1)}, bf16[64,2048]{1,0:T(8,128)(2,1)S(1)}, u32[]{:S(2)}, u32[]{:S(2)}) %collective-permute-start) | collective-permute-done | bytes 262176 | tf_op jit(solution)/shard_map/ppermute | solution.py:26
  89.3 4.7 collective-permute-done.1.hk_ref.hv_ref
  94.0 13.1 %shard_map.162 = (bf16[1024,1024]{1,0:T(8,128)(2,1)S(1)}, f32[8,8,256]{2,1,0:T(8,128)S(1)}) custom-call(bf16[1024,3072]{1,0:T(8,128)(2,1)} %shard_map.161.q_ref.k_ref.v_ref, bf16[1024,3072]{1,0:T(8,128)(2,1)} %shard_map.161.q_ref.k_ref.v_ref, bf16[1024,3072]{1,0:T(8,128)(2,1)} %shard_map.161.q_ref.k_ref.v_ref, ...), custom_call_target="tpu_custom_call" | custom-call | flops 4294967296 | bytes 8388608 | tf_op jit(solution)/shard_map/pallas_call | solution.py:149
  109.4 5.4 fusion.47
  117.4 44.9 %all-gather.9.cloned.1.call-done = bf16[1024,5248]{1,0:T(8,128)(2,1)} async-done(((bf16[256,5248]{1,0:T(8,128)(2,1)}), bf16[1024,5248]{1,0:T(8,128)(2,1)}) %all-gather.9.cloned.1.call-update) | async-done | bytes 10747920 | tf_op jit(solution)/shard_map/all_gather | solution.py:333
  162.3 20.8 %fusion.43 = f32[1024,5248]{1,0:T(8,128)} fusion(bf16[1024,5248]{1,0:T(8,128)(2,1)} %all-gather.9.cloned.1.call-done, f32[1024,1024]{1,0:T(8,128)} %copy-done.11, f32[1024]{0:T(1024)S(1)} %bitcast.88, f32[1024]{0:T(1024)S(1)} %add_rsqrt_fusion, f32[1024]{0:T(1024)S(1)} %broadcast_multiply_fusion.4), kind=kOutput, calls=%fused_computation.194 | convolution fusion | flops 11010048000 | bytes 36450304 | tf_op jit(solution)/shard_map/dot_general | solution.py:435
  183.0 22.4 %all-gather.11.cloned.1.call-done = bf16[2624,1024]{1,0:T(8,128)(2,1)} async-done(((bf16[656,1024]{1,0:T(8,128)(2,1)}), bf16[2624,1024]{1,0:T(8,128)(2,1)}) %all-gather.11.cloned.1.call-update) | async-done | bytes 5373968 | tf_op jit(solution)/shard_map/all_gather | solution.py:333
  205.5 37.5 %add_convert_fusion = (bf16[1024,2624]{1,0:T(8,128)(2,1)}, f32[1024,2624]{1,0:T(8,128)}, f32[2624,1024]{0,1:T(8,128)}) fusion(f32[1024,5248]{1,0:T(8,128)} %fusion.43, bf16[2624,1024]{1,0:T(8,128)(2,1)} %all-gather.11.cloned.1.call-done, bf16[1024,1024]{1,0:T(8,128)(2,1)} %param.19), kind=kOutput, calls=%fused_computation.6 | convolution fusion | flops 5699076096 | bytes 55836672 | tf_op jit(solution)/shard_map/nd,fd->nf/dot_general | solution.py:442
  242.9 17.6 %fusion.1 = (bf16[1024,2624]{1,0:T(8,128)(2,1)S(1)}, bf16[1024,2624]{1,0:T(8,128)(2,1)}) fusion(f32[2624,1024]{0,1:T(8,128)} %get-tuple-element.109, f32[1024,2624]{1,0:T(8,128)} %get-tuple-element.55, f32[1024,5248]{1,0:T(8,128)} %fusion.43), kind=kLoop, calls=%fused_computation.5 | loop fusion | flops 16121856 | bytes 53739520 | tf_op jit(solution)/shard_map/convert.5
  260.6 9.5 %pad_maximum_fusion = bf16[1024,5248]{1,0:T(8,128)(2,1)} fusion(bf16[1024,2624]{1,0:T(8,128)(2,1)S(1)} %get-tuple-element.56, bf16[1024,2624]{1,0:T(8,128)(2,1)} %get-tuple-element.54), kind=kLoop, calls=%fused_computation.21 | loop fusion | flops 21495808 | bytes 21495808 | tf_op jit(solution)/shard_map/concatenate | solution.py:444
  270.1 18.6 %convolution_convert_fusion = bf16[1024,5248]{1,0:T(8,128)(2,1)} fusion(bf16[1024,5248]{1,0:T(8,128)(2,1)} %pad_maximum_fusion, f32[1024,1024]{1,0:T(8,128)S(1)} %copy-done.12, f32[1024]{0:T(1024)S(1)} %bitcast.89, f32[1024]{0:T(1024)S(1)} %add_rsqrt_fusion, f32[1024]{0:T(1024)S(1)} %broadcast_multiply_fusion.4), kind=kOutput, calls=%fused_computation.1 | convolution fusion | flops 11015421952 | bytes 25702400 | tf_op jit(solution)/shard_map/nd,nf->df/dot_general | solution.py:445
  288.7 10.7 %convolution_convert_fusion.2 = bf16[2624,1024]{1,0:T(8,128)(2,1)} fusion(bf16[1024,2624]{1,0:T(8,128)(2,1)} %get-tuple-element.57, bf16[1024,1024]{1,0:T(8,128)(2,1)S(1)} %copy-done.15), kind=kOutput, calls=%fused_computation.30 | convolution fusion | flops 5505613824 | bytes 12845056 | tf_op jit(solution)/shard_map/nf,nd->fd/dot_general | solution.py:439
  302.4 19.5 %multiply_reduce_fusion = (f32[1024]{0:T(1024)S(1)}, f32[1024]{0:T(1024)S(1)}, f32[1024]{0:T(1024)S(1)}, f32[1024,1024]{1,0:T(8,128)}) fusion(f32[1024,1024]{1,0:T(8,128)S(1)} %copy-done.12, f32[1024]{0:T(1024)S(1)} %add_rsqrt_fusion, f32[1024]{0:T(1024)S(1)} %broadcast_multiply_fusion.4, f32[1024]{0:T(1024)S(1)} %bitcast.90, ...), kind=kOutput, calls=%fused_computation.47 | convolution fusion | flops 11014239232 | bytes 29908992 | tf_op jit(solution)/shard_map/nf,df->nd/dot_general | solution.py:448
  321.8 3.6 multiply_add_fusion
  330.7 3.7 convolution_convert_fusion.4.do_ref
  334.4 7.3 %add_convert_fusion.5 = bf16[1024,1024]{1,0:T(8,128)(2,1)} fusion(f32[1024,1024]{1,0:T(8,128)S(1)} %copy-done.12, bf16[1024,2624]{1,0:T(8,128)(2,1)S(1)} %bitcast.70, bf16[2624,1024]{1,0:T(8,128)(2,1)S(1)} %bitcast.103), kind=kOutput, calls=%fused_computation.50 | convolution fusion | flops 5505024000 | bytes 17039360 | tf_op jit(solution)/shard_map/dot_general | solution.py:441
  343.1 5.4 add_convert_fusion.1
  350.5 27.1 %shard_map.163 = (bf16[1024,1024]{1,0:T(8,128)(2,1)S(1)}, f32[1024,1024]{1,0:T(8,128)}, f32[1024,1024]{1,0:T(8,128)}, bf16[64,1024]{1,0:T(8,128)(2,1)S(1)}, bf16...) custom-call(bf16[1024,3072]{1,0:T(8,128)(2,1)} %shard_map.161.q_ref.k_ref.v_ref, ...), custom_call_target="tpu_custom_call" | custom-call | flops 10737418240 | bytes 20971520 | tf_op jit(solution)/shard_map/pallas_call | solution.py:226
  378.9 4.6 collective-permute-start.4
  388.1 29.0 %collective-permute-done.5.hi_ref = bf16[64,2048]{1,0:T(8,128)(2,1)S(1)} collective-permute-done((bf16[64,2048]{1,0:T(8,128)(2,1)S(1)}, bf16[64,2048]{1,0:T(8,128)(2,1)S(1)}, u32[]{:S(2)}, u32[]{:S(2)}) %collective-permute-start.5) | collective-permute-done | bytes 262176 | tf_op jit(solution)/shard_map/ppermute | solution.py:26
  417.7 16.5 %shard_map.164 = bf16[1024,3072]{1,0:T(8,128)(2,1)} custom-call(bf16[1024,1024]{1,0:T(8,128)(2,1)S(1)} %get-tuple-element.34.dq_ref, f32[1024,1024]{1,0:T(8,128)} %get-tuple-element.35.dk_ref, f32[1024,1024]{1,0:T(8,128)} %get-tuple-element.36.dv_ref, bf16[64,2048]{1,0:T(8,128)(2,1)S(1)} %collective-permute-done.4.lo_ref, ...), custom_call_target="tpu_custom_call" | custom-call | flops 8388608 | bytes 16777216 | tf_op jit(solution)/shard_map/pallas_call | solution.py:286
  434.2 11.4 %convolution_convert_fusion.1 = bf16[1024,3072]{1,0:T(8,128)(2,1)} fusion(bf16[1024,1024]{1,0:T(8,128)(2,1)S(1)} %fusion.14.act_ref, bf16[1024,3072]{1,0:T(8,128)(2,1)} %shard_map.164), kind=kOutput, calls=%fused_computation.29 | convolution fusion | flops 6445596672 | bytes 14680064 | tf_op jit(solution)/shard_map/nd,nf->df/dot_general | solution.py:472
  445.7 5.3 collective-permute-done.7
  459.7 9.6 %fusion.19 = (f32[1024]{0:T(1024)S(1)}, f32[1024]{0:T(1024)S(1)}, f32[1024]{0:T(1024)S(1)}, f32[1024,1024]{1,0:T(8,128)S(1)}) fusion(bf16[1024,1024]{1,0:T(8,128)(2,1)S(1)} %copy-done.8, f32[1024]{0:T(1024)S(1)} %copy-done.21, f32[1024]{0:T(1024)S(1)} %copy-done.19, f32[1024]{0:T(1024)S(1)} %bitcast.79, bf16[1024,3072]{1,0:T(8,128)(2,1)S(1)} %bitcast.64, ...), kind=kOutput, calls=%fused_computation.45 | convolution fusion | flops 6451885056 | bytes 18898944 | tf_op jit(solution)/shard_map/nf,df->nd/dot_general | solution.py:478
  472.2 30.0 %collective-permute-done.10 = f32[2,1024]{1,0:T(2,128)S(1)} collective-permute-done((f32[2,1024]{1,0:T(2,128)S(1)}, f32[2,1024]{1,0:T(2,128)S(1)}, u32[]{:S(2)}, u32[]{:S(2)}) %collective-permute-start.10) | collective-permute-done | bytes 8224 | tf_op jit(solution)/shard_map/ppermute | solution.py:385
  513.4 3.2 fusion.18
  522.8 3.7 collective-permute-done.25
  529.4 3.2 collective-permute-done.26
  537.9 5.5 collective-permute-start.28
  543.4 3.6 collective-permute-done.40
  556.8 15.9 %collective-permute-done.42 = bf16[656,256]{1,0:T(8,128)(2,1)S(1)} collective-permute-done((bf16[656,256]{1,0:T(8,128)(2,1)S(1)}, bf16[656,256]{1,0:T(8,128)(2,1)S(1)}, u32[]{:S(2)}, u32[]{:S(2)}) %collective-permute-start.42) | collective-permute-done | bytes 335904 | tf_op jit(solution)/shard_map/ppermute | solution.py:355
  575.6 16.8 %collective-permute-done.33 = bf16[32,5248]{1,0:T(8,128)(2,1)S(1)} collective-permute-done((bf16[32,5248]{1,0:T(8,128)(2,1)S(1)}, bf16[32,5248]{1,0:T(8,128)(2,1)S(1)}, u32[]{:S(2)}, u32[]{:S(2)}) %collective-permute-start.33) | collective-permute-done | bytes 335904 | tf_op jit(solution)/shard_map/ppermute | solution.py:350
  594.1 6.7 collective-permute-done.34
  601.0 18.9 %collective-permute-done.15 = bf16[1,256,3072]{2,1,0:T(8,128)(2,1)S(1)} collective-permute-done((bf16[1,256,3072]{2,1,0:T(8,128)(2,1)S(1)}, bf16[1,256,3072]{2,1,0:T(8,128)(2,1)S(1)}, u32[]{:S(2)}, u32[]{:S(2)}) %collective-permute-start.15) | collective-permute-done | bytes 1572896 | tf_op jit(solution)/shard_map/ppermute | solution.py:350
  620.9 11.7 %collective-permute-done.16 = bf16[128,3072]{1,0:T(8,128)(2,1)S(1)} collective-permute-done((bf16[128,3072]{1,0:T(8,128)(2,1)S(1)}, bf16[128,3072]{1,0:T(8,128)(2,1)S(1)}, u32[]{:S(2)}, u32[]{:S(2)}) %collective-permute-start.16) | collective-permute-done | bytes 786464 | tf_op jit(solution)/shard_map/ppermute | solution.py:350
  632.8 10.0 %collective-permute-start.17 = (bf16[64,3072]{1,0:T(8,128)(2,1)S(1)}, bf16[64,3072]{1,0:T(8,128)(2,1)S(1)}, u32[]{:S(2)}, u32[]{:S(2)}) collective-permute-start(bf16[64,3072]{1,0:T(8,128)(2,1)S(1)} %constant_dynamic-slice_fusion.10), channel_id=1, source_target_pairs={{0,8},{2,10},{4,12},{6,14},{8,0},{10,2},{12,4},{14,6},{16,24},{18,... | collective-permute-start | bytes 1179656 | tf_op jit(solution)/shard_map/ppermute | solution.py:350
  645.0 5.7 collective-permute-done.17
  651.7 11.6 %collective-permute-done.18 = bf16[32,3072]{1,0:T(8,128)(2,1)S(1)} collective-permute-done((bf16[32,3072]{1,0:T(8,128)(2,1)S(1)}, bf16[32,3072]{1,0:T(8,128)(2,1)S(1)}, u32[]{:S(2)}, u32[]{:S(2)}) %collective-permute-start.18) | collective-permute-done | bytes 196640 | tf_op jit(solution)/shard_map/ppermute | solution.py:350
  663.4 3.8 collective-permute-done.36
  667.6 3.9 collective-permute-done.19
  671.9 7.5 %collective-permute-done.20 = bf16[64,3072]{1,0:T(8,128)(2,1)S(1)} collective-permute-done((bf16[64,3072]{1,0:T(8,128)(2,1)S(1)}, bf16[64,3072]{1,0:T(8,128)(2,1)S(1)}, u32[]{:S(2)}, u32[]{:S(2)}) %collective-permute-start.20) | collective-permute-done | bytes 393248 | tf_op jit(solution)/shard_map/ppermute | solution.py:355
  686.9 5.4 collective-permute-done.21
  693.8 4.9 maximum_convert_fusion
  699.5 3.5 maximum_convert_fusion.1
  (268 shorter events, 110.2 us)
Async XLA Ops:
  7.2 52.4 %all-gather.5.cloned.1.call-start = ((), (), s32[]{:S(2)}) async-start(), calls=%async_computation | async-start | bytes 7864320 | tf_op jit(solution)/shard_map/all_gather | solution.py:333
  10.3 99.1 %all-gather.7.cloned.1.call-start = ((), (), s32[]{:S(2)}) async-start(), calls=%async_computation.1 | async-start | bytes 2621440 | tf_op jit(solution)/shard_map/all_gather | solution.py:333
  12.3 150.0 %all-gather.9.cloned.1.call-start = ((), (), s32[]{:S(2)}) async-start(), calls=%async_computation.2 | async-start | bytes 13434880 | tf_op jit(solution)/shard_map/all_gather | solution.py:333
  15.8 189.6 %all-gather.11.cloned.1.call-start = ((), (), s32[]{:S(2)}) async-start(), calls=%async_computation.3 | async-start | bytes 6717440 | tf_op jit(solution)/shard_map/all_gather | solution.py:333
  76.1 13.2 %collective-permute-start = (bf16[64,2048]{1,0:T(8,128)(2,1)}, bf16[64,2048]{1,0:T(8,128)(2,1)S(1)}, u32[]{:S(2)}, u32[]{:S(2)}) collective-permute-start(bf16[64,2048]{1,0:T(8,128)(2,1)} %get-tuple-element.59), channel_id=1, source_target_pairs={{0,1},{1,2},{2,3},{3,4},{4,5},{5,6},{6,7},{7,8},{8,9},{9,10},{10,1... | collective-permute-start | bytes 786440 | tf_op jit(solution)/shard_map/ppermute | solution.py:26
  78.3 15.7 %collective-permute-start.1 = (bf16[64,2048]{1,0:T(8,128)(2,1)}, bf16[64,2048]{1,0:T(8,128)(2,1)}, u32[]{:S(2)}, u32[]{:S(2)}) collective-permute-start(bf16[64,2048]{1,0:T(8,128)(2,1)} %get-tuple-element.58), channel_id=1, source_target_pairs={{1,0},{2,1},{3,2},{4,3},{5,4},{6,5},{7,6},{8,7},{9,8},{10,9},{11,1... | collective-permute-start | bytes 786440 | tf_op jit(solution)/shard_map/ppermute | solution.py:26
  302.1 41.0 %collective-permute-start.2 = (bf16[2,256,5248]{2,1,0:T(8,128)(2,1)}, bf16[2,256,5248]{2,1,0:T(8,128)(2,1)}, u32[]{:S(2)}, u32[]{:S(2)}) collective-permute-start(bf16[2,256,5248]{2,1,0:T(8,128)(2,1)} %constant_dynamic-slice_fusion.19), channel_id=1, source_target_pairs={{0,2},{2,0},{4,6},{6,4},{8,10},{10,8},{12,14},{14,12},{16,18},{18,... | collective-permute-start | bytes 16121864 | tf_op jit(solution)/shard_map/ppermute | solution.py:350
  329.0 54.4 %collective-permute-start.8 = (bf16[2,256,1024]{2,1,0:T(8,128)(2,1)}, bf16[2,256,1024]{2,1,0:T(8,128)(2,1)}, u32[]{:S(2)}, u32[]{:S(2)}) collective-permute-start(bf16[2,256,1024]{2,1,0:T(8,128)(2,1)} %constant_dynamic-slice_fusion.15), channel_id=1, source_target_pairs={{0,2},{2,0},{4,6},{6,4},{8,10},{10,8},{12,14},{14,12},{16,18},{18,... | collective-permute-start | bytes 3145736 | tf_op jit(solution)/shard_map/ppermute | solution.py:350
  330.0 11.8 %collective-permute-start.3 = (bf16[2,656,1024]{2,1,0:T(8,128)(2,1)S(1)}, bf16[2,656,1024]{2,1,0:T(8,128)(2,1)S(1)}, u32[]{:S(2)}, u32[]{:S(2)}) collective-permute-start(bf16[2,656,1024]{2,1,0:T(8,128)(2,1)S(1)} %constant_dynamic-slice_fusion.18), channel_id=1, source_target_pairs={{0,2},{2,0},{4,6},{6,4},{8,10},{10,8},{12,14},{14,12},{16,18},{18,... | collective-permute-start | bytes 8060936 | tf_op jit(solution)/shard_map/ppermute | solution.py:350
  350.2 102.9 %collective-permute-start.6 = (bf16[1,256,5248]{2,1,0:T(8,128)(2,1)}, bf16[1,256,5248]{2,1,0:T(8,128)(2,1)}, u32[]{:S(2)}, u32[]{:S(2)}) collective-permute-start(bf16[1,256,5248]{2,1,0:T(8,128)(2,1)} %constant_dynamic-slice_fusion.17), channel_id=1, source_target_pairs={{0,1},{1,0},{2,3},{3,2},{4,5},{5,4},{6,7},{7,6},{8,9},{9,8},{10,11... | collective-permute-start | bytes 8060936 | tf_op jit(solution)/shard_map/ppermute | solution.py:350
  377.6 39.5 %collective-permute-start.5 = (bf16[64,2048]{1,0:T(8,128)(2,1)S(1)}, bf16[64,2048]{1,0:T(8,128)(2,1)S(1)}, u32[]{:S(2)}, u32[]{:S(2)}) collective-permute-start(bf16[64,2048]{1,0:T(8,128)(2,1)S(1)} %pad_maximum_fusion.14), channel_id=1, source_target_pairs={{1,0},{2,1},{3,2},{4,3},{5,4},{6,5},{7,6},{8,7},{9,8},{10,9},{11,1... | collective-permute-start | bytes 786440 | tf_op jit(solution)/shard_map/ppermute | solution.py:26
  378.9 38.8 %collective-permute-start.4 = (bf16[64,2048]{1,0:T(8,128)(2,1)S(1)}, bf16[64,2048]{1,0:T(8,128)(2,1)S(1)}, u32[]{:S(2)}, u32[]{:S(2)}) collective-permute-start(bf16[64,2048]{1,0:T(8,128)(2,1)S(1)} %pad_maximum_fusion.13), channel_id=1, source_target_pairs={{0,1},{1,2},{2,3},{3,4},{4,5},{5,6},{6,7},{7,8},{8,9},{9,10},{10,1... | collective-permute-start | bytes 786440 | tf_op jit(solution)/shard_map/ppermute | solution.py:26
  386.6 64.3 %collective-permute-start.7 = (bf16[1,656,1024]{2,1,0:T(8,128)(2,1)S(1)}, bf16[1,656,1024]{2,1,0:T(8,128)(2,1)}, u32[]{:S(2)}, u32[]{:S(2)}) collective-permute-start(bf16[1,656,1024]{2,1,0:T(8,128)(2,1)S(1)} %constant_dynamic-slice_fusion.16), channel_id=1, source_target_pairs={{0,1},{1,0},{2,3},{3,2},{4,5},{5,4},{6,7},{7,6},{8,9},{9,8},{10,11... | collective-permute-start | bytes 4030472 | tf_op jit(solution)/shard_map/ppermute | solution.py:350
  456.5 64.9 %collective-permute-start.38 = (bf16[656,512]{1,0:T(8,128)(2,1)}, bf16[656,512]{1,0:T(8,128)(2,1)}, u32[]{:S(2)}, u32[]{:S(2)}) collective-permute-start(bf16[656,512]{1,0:T(8,128)(2,1)} %constant_dynamic-slice_fusion.2), channel_id=1, source_target_pairs={{0,4},{2,6},{4,0},{6,2},{8,12},{10,14},{12,8},{14,10},{16,20},{18,... | collective-permute-start | bytes 2015240 | tf_op jit(solution)/shard_map/ppermute | solution.py:350
  457.6 92.6 %collective-permute-start.31 = (bf16[128,5248]{1,0:T(8,128)(2,1)}, bf16[128,5248]{1,0:T(8,128)(2,1)}, u32[]{:S(2)}, u32[]{:S(2)}) collective-permute-start(bf16[128,5248]{1,0:T(8,128)(2,1)} %constant_dynamic-slice_fusion.5), channel_id=1, source_target_pairs={{0,4},{2,6},{4,0},{6,2},{8,12},{10,14},{12,8},{14,10},{16,20},{18,... | collective-permute-start | bytes 4030472 | tf_op jit(solution)/shard_map/ppermute | solution.py:350
  469.5 43.0 %collective-permute-start.23 = (bf16[1,256,1024]{2,1,0:T(8,128)(2,1)S(1)}, bf16[1,256,1024]{2,1,0:T(8,128)(2,1)S(1)}, u32[]{:S(2)}, u32[]{:S(2)}) collective-permute-start(bf16[1,256,1024]{2,1,0:T(8,128)(2,1)S(1)} %constant_dynamic-slice_fusion.8), channel_id=1, source_target_pairs={{0,1},{1,0},{2,3},{3,2},{4,5},{5,4},{6,7},{7,6},{8,9},{9,8},{10,11... | collective-permute-start | bytes 1572872 | tf_op jit(solution)/shard_map/ppermute | solution.py:350
  470.7 31.5 %collective-permute-start.10 = (f32[2,1024]{1,0:T(2,128)S(1)}, f32[2,1024]{1,0:T(2,128)S(1)}, u32[]{:S(2)}, u32[]{:S(2)}) collective-permute-start(f32[2,1024]{1,0:T(2,128)S(1)} %fusion.42), channel_id=1, source_target_pairs={{0,4},{2,6},{4,0},{6,2},{8,12},{10,14},{12,8},{14,10},{16,20},{18,... | collective-permute-start | bytes 24584 | tf_op jit(solution)/shard_map/ppermute | solution.py:385
  472.2 120.5 %collective-permute-start.14 = (bf16[2,256,3072]{2,1,0:T(8,128)(2,1)S(1)}, bf16[2,256,3072]{2,1,0:T(8,128)(2,1)S(1)}, u32[]{:S(2)}, u32[]{:S(2)}) collective-permute-start(bf16[2,256,3072]{2,1,0:T(8,128)(2,1)S(1)} %constant_dynamic-slice_fusion.12), channel_id=1, source_target_pairs={{0,2},{2,0},{4,6},{6,4},{8,10},{10,8},{12,14},{14,12},{16,18},{18,... | collective-permute-start | bytes 9437192 | tf_op jit(solution)/shard_map/ppermute | solution.py:350
  502.2 3.8 collective-permute-start.11
  506.0 4.5 collective-permute-start.12
  510.6 6.0 collective-permute-start.13
  512.7 6.4 collective-permute-start.24
  519.3 7.2 %collective-permute-start.25 = (bf16[64,1024]{1,0:T(8,128)(2,1)S(1)}, bf16[64,1024]{1,0:T(8,128)(2,1)S(1)}, u32[]{:S(2)}, u32[]{:S(2)}) collective-permute-start(bf16[64,1024]{1,0:T(8,128)(2,1)S(1)} %constant_dynamic-slice_fusion.7), channel_id=1, source_target_pairs={{0,8},{2,10},{4,12},{6,14},{8,0},{10,2},{12,4},{14,6},{16,24},{18,... | collective-permute-start | bytes 393224 | tf_op jit(solution)/shard_map/ppermute | solution.py:350
  522.7 12.1 %collective-permute-start.39 = (bf16[656,256]{1,0:T(8,128)(2,1)S(1)}, bf16[656,256]{1,0:T(8,128)(2,1)S(1)}, u32[]{:S(2)}, u32[]{:S(2)}) collective-permute-start(bf16[656,256]{1,0:T(8,128)(2,1)S(1)} %constant_dynamic-slice_fusion.1), channel_id=1, source_target_pairs={{0,8},{2,10},{4,12},{6,14},{8,0},{10,2},{12,4},{14,6},{16,24},{18,... | collective-permute-start | bytes 1007624 | tf_op jit(solution)/shard_map/ppermute | solution.py:350
  526.5 6.0 collective-permute-start.26
  532.6 5.3 collective-permute-start.27
  534.9 12.1 %collective-permute-start.40 = (bf16[656,128]{1,0:T(8,128)(2,1)S(1)}, bf16[656,128]{1,0:T(8,128)(2,1)S(1)}, u32[]{:S(2)}, u32[]{:S(2)}) collective-permute-start(bf16[656,128]{1,0:T(8,128)(2,1)S(1)} %constant_dynamic-slice_fusion), channel_id=1, source_target_pairs={{0,16},{2,18},{4,20},{6,22},{8,24},{10,26},{12,28},{14,30},{16,0},... | collective-permute-start | bytes 503816 | tf_op jit(solution)/shard_map/ppermute | solution.py:350
  537.9 12.1 %collective-permute-start.28 = (bf16[64,1024]{1,0:T(8,128)(2,1)S(1)}, bf16[64,1024]{1,0:T(8,128)(2,1)S(1)}, u32[]{:S(2)}, u32[]{:S(2)}) collective-permute-start(bf16[64,1024]{1,0:T(8,128)(2,1)S(1)} %pad_maximum_fusion.16), channel_id=1, source_target_pairs={{0,8},{2,10},{4,12},{6,14},{8,0},{10,2},{12,4},{14,6},{16,24},{18,... | collective-permute-start | bytes 393224 | tf_op jit(solution)/shard_map/ppermute | solution.py:355
  547.1 7.9 %collective-permute-start.41 = (bf16[656,128]{1,0:T(8,128)(2,1)S(1)}, bf16[656,128]{1,0:T(8,128)(2,1)S(1)}, u32[]{:S(2)}, u32[]{:S(2)}) collective-permute-start(bf16[656,128]{1,0:T(8,128)(2,1)S(1)} %add_convert_fusion.17), channel_id=1, source_target_pairs={{0,16},{2,18},{4,20},{6,22},{8,24},{10,26},{12,28},{14,30},{16,0},... | collective-permute-start | bytes 503816 | tf_op jit(solution)/shard_map/ppermute | solution.py:355
  550.1 6.4 collective-permute-start.29
  551.9 20.9 %collective-permute-start.32 = (bf16[64,5248]{1,0:T(8,128)(2,1)S(1)}, bf16[64,5248]{1,0:T(8,128)(2,1)S(1)}, u32[]{:S(2)}, u32[]{:S(2)}) collective-permute-start(bf16[64,5248]{1,0:T(8,128)(2,1)S(1)} %constant_dynamic-slice_fusion.4), channel_id=1, source_target_pairs={{0,8},{2,10},{4,12},{6,14},{8,0},{10,2},{12,4},{14,6},{16,24},{18,... | collective-permute-start | bytes 2015240 | tf_op jit(solution)/shard_map/ppermute | solution.py:350
  555.0 17.6 %collective-permute-start.42 = (bf16[656,256]{1,0:T(8,128)(2,1)S(1)}, bf16[656,256]{1,0:T(8,128)(2,1)S(1)}, u32[]{:S(2)}, u32[]{:S(2)}) collective-permute-start(bf16[656,256]{1,0:T(8,128)(2,1)S(1)} %pad_maximum_fusion.12), channel_id=1, source_target_pairs={{0,8},{2,10},{4,12},{6,14},{8,0},{10,2},{12,4},{14,6},{16,24},{18,... | collective-permute-start | bytes 1007624 | tf_op jit(solution)/shard_map/ppermute | solution.py:355
  556.7 18.6 %collective-permute-start.30 = (bf16[256,1024]{1,0:T(8,128)(2,1)S(1)}, bf16[256,1024]{1,0:T(8,128)(2,1)S(1)}, u32[]{:S(2)}, u32[]{:S(2)}) collective-permute-start(bf16[256,1024]{1,0:T(8,128)(2,1)S(1)} %pad_maximum_fusion.10), channel_id=1, source_target_pairs={{0,2},{2,0},{4,6},{6,4},{8,10},{10,8},{12,14},{14,12},{16,18},{18,... | collective-permute-start | bytes 1572872 | tf_op jit(solution)/shard_map/ppermute | solution.py:355
  573.1 19.4 %collective-permute-start.33 = (bf16[32,5248]{1,0:T(8,128)(2,1)S(1)}, bf16[32,5248]{1,0:T(8,128)(2,1)S(1)}, u32[]{:S(2)}, u32[]{:S(2)}) collective-permute-start(bf16[32,5248]{1,0:T(8,128)(2,1)S(1)} %constant_dynamic-slice_fusion.3), channel_id=1, source_target_pairs={{0,16},{2,18},{4,20},{6,22},{8,24},{10,26},{12,28},{14,30},{16,0},... | collective-permute-start | bytes 1007624 | tf_op jit(solution)/shard_map/ppermute | solution.py:350
  573.3 77.9 %collective-permute-start.43 = (bf16[656,512]{1,0:T(8,128)(2,1)S(1)}, bf16[656,512]{1,0:T(8,128)(2,1)S(1)}, u32[]{:S(2)}, u32[]{:S(2)}) collective-permute-start(bf16[656,512]{1,0:T(8,128)(2,1)S(1)} %pad_maximum_fusion.7), channel_id=1, source_target_pairs={{0,4},{2,6},{4,0},{6,2},{8,12},{10,14},{12,8},{14,10},{16,20},{18,... | collective-permute-start | bytes 2015240 | tf_op jit(solution)/shard_map/ppermute | solution.py:355
  592.5 8.2 %collective-permute-start.34 = (bf16[32,5248]{1,0:T(8,128)(2,1)S(1)}, bf16[32,5248]{1,0:T(8,128)(2,1)S(1)}, u32[]{:S(2)}, u32[]{:S(2)}) collective-permute-start(bf16[32,5248]{1,0:T(8,128)(2,1)S(1)} %add_convert_fusion.15), channel_id=1, source_target_pairs={{0,16},{2,18},{4,20},{6,22},{8,24},{10,26},{12,28},{14,30},{16,0},... | collective-permute-start | bytes 1007624 | tf_op jit(solution)/shard_map/ppermute | solution.py:355
  593.9 26.0 %collective-permute-start.15 = (bf16[1,256,3072]{2,1,0:T(8,128)(2,1)S(1)}, bf16[1,256,3072]{2,1,0:T(8,128)(2,1)S(1)}, u32[]{:S(2)}, u32[]{:S(2)}) collective-permute-start(bf16[1,256,3072]{2,1,0:T(8,128)(2,1)S(1)} %constant_dynamic-slice_fusion.11), channel_id=1, source_target_pairs={{0,1},{1,0},{2,3},{3,2},{4,5},{5,4},{6,7},{7,6},{8,9},{9,8},{10,11... | collective-permute-start | bytes 4718600 | tf_op jit(solution)/shard_map/ppermute | solution.py:350
  600.9 19.7 %collective-permute-start.35 = (bf16[64,5248]{1,0:T(8,128)(2,1)S(1)}, bf16[64,5248]{1,0:T(8,128)(2,1)S(1)}, u32[]{:S(2)}, u32[]{:S(2)}) collective-permute-start(bf16[64,5248]{1,0:T(8,128)(2,1)S(1)} %pad_maximum_fusion.6), channel_id=1, source_target_pairs={{0,8},{2,10},{4,12},{6,14},{8,0},{10,2},{12,4},{14,6},{16,24},{18,... | collective-permute-start | bytes 2015240 | tf_op jit(solution)/shard_map/ppermute | solution.py:355
  620.5 12.1 %collective-permute-start.16 = (bf16[128,3072]{1,0:T(8,128)(2,1)S(1)}, bf16[128,3072]{1,0:T(8,128)(2,1)S(1)}, u32[]{:S(2)}, u32[]{:S(2)}) collective-permute-start(bf16[128,3072]{1,0:T(8,128)(2,1)S(1)} %dynamic-slice_bitcast_fusion), channel_id=1, source_target_pairs={{0,4},{2,6},{4,0},{6,2},{8,12},{10,14},{12,8},{14,10},{16,20},{18,... | collective-permute-start | bytes 2359304 | tf_op jit(solution)/shard_map/ppermute | solution.py:350
  632.8 17.8 %collective-permute-start.17 = (bf16[64,3072]{1,0:T(8,128)(2,1)S(1)}, bf16[64,3072]{1,0:T(8,128)(2,1)S(1)}, u32[]{:S(2)}, u32[]{:S(2)}) collective-permute-start(bf16[64,3072]{1,0:T(8,128)(2,1)S(1)} %constant_dynamic-slice_fusion.10), channel_id=1, source_target_pairs={{0,8},{2,10},{4,12},{6,14},{8,0},{10,2},{12,4},{14,6},{16,24},{18,... | collective-permute-start | bytes 1179656 | tf_op jit(solution)/shard_map/ppermute | solution.py:350
  642.9 24.3 %collective-permute-start.36 = (bf16[128,5248]{1,0:T(8,128)(2,1)S(1)}, bf16[128,5248]{1,0:T(8,128)(2,1)S(1)}, u32[]{:S(2)}, u32[]{:S(2)}) collective-permute-start(bf16[128,5248]{1,0:T(8,128)(2,1)S(1)} %pad_maximum_fusion.3), channel_id=1, source_target_pairs={{0,4},{2,6},{4,0},{6,2},{8,12},{10,14},{12,8},{14,10},{16,20},{18,... | collective-permute-start | bytes 4030472 | tf_op jit(solution)/shard_map/ppermute | solution.py:355
  650.8 12.5 %collective-permute-start.18 = (bf16[32,3072]{1,0:T(8,128)(2,1)S(1)}, bf16[32,3072]{1,0:T(8,128)(2,1)S(1)}, u32[]{:S(2)}, u32[]{:S(2)}) collective-permute-start(bf16[32,3072]{1,0:T(8,128)(2,1)S(1)} %constant_dynamic-slice_fusion.9), channel_id=1, source_target_pairs={{0,16},{2,18},{4,20},{6,22},{8,24},{10,26},{12,28},{14,30},{16,0},... | collective-permute-start | bytes 589832 | tf_op jit(solution)/shard_map/ppermute | solution.py:350
  651.6 31.5 %collective-permute-start.44 = (bf16[656,1024]{1,0:T(8,128)(2,1)S(1)}, bf16[656,1024]{1,0:T(8,128)(2,1)S(1)}, u32[]{:S(2)}, u32[]{:S(2)}) collective-permute-start(bf16[656,1024]{1,0:T(8,128)(2,1)S(1)} %pad_maximum_fusion.4), channel_id=1, source_target_pairs={{0,2},{2,0},{4,6},{6,4},{8,10},{10,8},{12,14},{14,12},{16,18},{18,... | collective-permute-start | bytes 4030472 | tf_op jit(solution)/shard_map/ppermute | solution.py:355
  663.3 8.2 %collective-permute-start.19 = (bf16[32,3072]{1,0:T(8,128)(2,1)S(1)}, bf16[32,3072]{1,0:T(8,128)(2,1)S(1)}, u32[]{:S(2)}, u32[]{:S(2)}) collective-permute-start(bf16[32,3072]{1,0:T(8,128)(2,1)S(1)} %add_convert_fusion.16), channel_id=1, source_target_pairs={{0,16},{2,18},{4,20},{6,22},{8,24},{10,26},{12,28},{14,30},{16,0},... | collective-permute-start | bytes 589832 | tf_op jit(solution)/shard_map/ppermute | solution.py:355
  671.6 7.8 %collective-permute-start.20 = (bf16[64,3072]{1,0:T(8,128)(2,1)S(1)}, bf16[64,3072]{1,0:T(8,128)(2,1)S(1)}, u32[]{:S(2)}, u32[]{:S(2)}) collective-permute-start(bf16[64,3072]{1,0:T(8,128)(2,1)S(1)} %pad_maximum_fusion.11), channel_id=1, source_target_pairs={{0,8},{2,10},{4,12},{6,14},{8,0},{10,2},{12,4},{14,6},{16,24},{18,... | collective-permute-start | bytes 1179656 | tf_op jit(solution)/shard_map/ppermute | solution.py:355
  671.8 21.0 %collective-permute-start.37 = (bf16[256,5248]{1,0:T(8,128)(2,1)S(1)}, bf16[256,5248]{1,0:T(8,128)(2,1)S(1)}, u32[]{:S(2)}, u32[]{:S(2)}) collective-permute-start(bf16[256,5248]{1,0:T(8,128)(2,1)S(1)} %pad_maximum_fusion.1), channel_id=1, source_target_pairs={{0,2},{2,0},{4,6},{6,4},{8,10},{10,8},{12,14},{14,12},{16,18},{18,... | collective-permute-start | bytes 8060936 | tf_op jit(solution)/shard_map/ppermute | solution.py:355
  679.6 12.7 %collective-permute-start.21 = (bf16[128,3072]{1,0:T(8,128)(2,1)S(1)}, bf16[128,3072]{1,0:T(8,128)(2,1)S(1)}, u32[]{:S(2)}, u32[]{:S(2)}) collective-permute-start(bf16[128,3072]{1,0:T(8,128)(2,1)S(1)} %pad_maximum_fusion.5), channel_id=1, source_target_pairs={{0,4},{2,6},{4,0},{6,2},{8,12},{10,14},{12,8},{14,10},{16,20},{18,... | collective-permute-start | bytes 2359304 | tf_op jit(solution)/shard_map/ppermute | solution.py:355
  692.8 5.9 collective-permute-start.22
  (39 other events, 255.5 us)
Sparse Core Ops, SparseCore 0:
  10.5 49.1 all-gather.4
  61.7 23.8 all-gather.6
  87.8 74.4 all-gather.8
  164.2 41.1 all-gather.10
